TPU v7x, 32 devices: a whole 2x2x4 slice. The times are simulated.
32 devices in a mesh: groups: 2 (over y), blk: 4 (over z), slab: 2 (over x), ch: 2 (over core).
Axes of the slice: x: 2, y: 2, z: 4, core: 2. Of those that a mesh axis runs over, the one named last changes fastest.
Arguments:
- fine_input: bfloat16 [8, 4, 4, 256, 128], P(('groups', 'slab', 'ch'), 'blk'), parts along dimension 0, may hold values from -6 to 6
- cotangent: bfloat16 [8, 4, 4, 256, 128], P(('groups', 'slab', 'ch'), 'blk'), parts along dimension 0, may hold values from -6 to 6
- conv_weight: bfloat16 [27, 128, 128], replicated, may hold values from -0.109375 to 0.109375
- down_weight: bfloat16 [128, 256], replicated, may hold values from -0.5 to 0.5
- depth_weight: bfloat16 [27, 256], replicated, may hold values from -1.25 to 1.25
- up_weight: bfloat16 [256, 128], replicated, may hold values from -0.375 to 0.375
- slot_x: int32 [8, 4, 4], P(('groups', 'slab', 'ch'), 'blk'), parts along dimension 0, may hold values from -1 to 11, as said below
- neighbours: int32 [8, 4, 4, 27], P(('groups', 'slab', 'ch'), 'blk'), parts along dimension 0, may hold values from -1 to 3, as said below
Outputs:
- input_grad: bfloat16 [8, 4, 4, 256, 128], P(('groups', 'slab', 'ch'), 'blk'), parts along dimension 0
- conv_grad: float32 [54, 16384], P('groups', ('blk', 'slab', 'ch')), parts along dimension 0
- down_grad: float32 [256, 256], P('groups'), parts along dimension 0
- depth_grad: float32 [54, 256], P('groups'), parts along dimension 0
- up_grad: float32 [512, 128], P('groups'), parts along dimension 0
There are 2 independent parts, one for each index of `groups`. A program takes and returns all parts, laid end to end along the dimension named above; an argument that names none is the same for every part. Nothing has to cross between parts.
Inputs may be any that keep to these rules, and one draw needn't show every extreme that they name: `slot_x`: each device row of 4 entries lists distinct x block indices, occupied slots first and -1 in the rest. Rows 2m and 2m + 1 of the first dimension hold the two z halves of the same blocks in the same slots. Some row holds 4 blocks. `neighbours`: entry 9a + 3b + e of slot k at row j, column i gives the slot, in row j + a - 1 and column i + b - 1, of the occupied block at x block index slot_x[j, i, k] + e - 1, or -1 where that block is unoccupied or outside the grid; every entry of an empty slot is -1.
All inputs are finite; a program needn't handle non-finite values.
Results may differ from a plain program's by a relative error of at most 0.0068.
Values may be sent and summed in bfloat16 or wider, within the bound.
A program may use at most 64 MiB of HBM per device.

v0:
```python
import jax
import jax.numpy as jnp
from jax import lax
from jax.sharding import PartitionSpec as P

GX = 12


def with_halo(shard, sides, width):
    for axis, dim in sides:
        size, length = (lax.axis_size(axis), shard.shape[dim])
        up = [(i, (i + 1) % size) for i in range(size - 1)]
        down = [(j, i) for i, j in up]
        last = lax.slice_in_dim(shard, length - width, length, axis=dim)
        leading = lax.slice_in_dim(shard, 0, width, axis=dim)
        before = lax.ppermute(last, axis, up)
        after = lax.ppermute(leading, axis, down)
        shard = jnp.concatenate([before, shard, after], axis=dim)
    return shard


def silu_slope(value):
    sigma = jax.nn.sigmoid(value)
    return sigma * (1.0 + value * (1.0 - sigma))


def tap_slice(tiles, index, flip):
    start_z, start_y, start_x = (index // 9, index // 3 % 3, index % 3)
    if flip:
        start_z, start_y, start_x = (2 - start_z, 2 - start_y, 2 - start_x)
    part = tiles[:, start_z : start_z + 4, start_y : start_y + 8, start_x : start_x + 8]
    return part.reshape(tiles.shape[0] * 256, tiles.shape[-1])


def fine_tiles(volume, place):
    chans = volume.shape[-1]
    select = (place[:, None] == jnp.arange(GX, dtype=jnp.int32)[None, :]).astype(volume.dtype)
    dense = jnp.einsum(
        "kg,kzyxc->zygxc", select, volume, preferred_element_type=jnp.float32
    ).astype(volume.dtype)
    dense = dense.reshape(4, 8, GX * 8, chans)
    framed = with_halo(dense, (("blk", 1), (("slab", "ch"), 0)), 1)
    framed = jnp.pad(framed, ((0, 0), (0, 0), (1, 1), (0, 0)))
    anchor = jnp.zeros((), jnp.int32)

    def cut_tile(start):
        return lax.dynamic_slice(framed, (anchor, anchor, start, anchor), (6, 10, 10, chans))

    return jax.vmap(cut_tile)(8 * jnp.maximum(place, 0))


def coarse_frame(grid):
    framed = with_halo(grid, (("blk", 1), (("slab", "ch"), 0)), 1)
    return jnp.pad(framed, ((0, 0), (0, 0), (1, 1), (0, 0)))


def coarse_spread(framed, depth, flip, span):
    total = jnp.zeros((1, 2, span, depth.shape[1]), jnp.float32)
    for index in range(27):
        start_z, start_y, start_x = (index // 9, index // 3 % 3, index % 3)
        if flip:
            start_z, start_y, start_x = (2 - start_z, 2 - start_y, 2 - start_x)
        total = (
            total
            + framed[start_z : start_z + 1, start_y : start_y + 2, start_x : start_x + span].astype(
                jnp.float32
            )
            * depth[index]
        )
    return total


def per_device(
    fine_input, cotangent, conv_weight, down_weight, depth_weight, up_weight, slot_x, neighbours
):
    slots = fine_input.shape[2]
    chans = fine_input.shape[4]
    wide = down_weight.shape[1]
    span = 2 * GX
    cells = 2 * span
    place = slot_x[0, 0]
    livef = (place >= 0).astype(jnp.float32)[:, None, None]
    select = (place[:, None] == jnp.arange(GX, dtype=jnp.int32)[None, :]).astype(jnp.float32)
    volume = fine_input[0, 0].reshape(slots, 4, 8, 8, chans)
    tiles = fine_tiles(volume, place)
    field = jnp.zeros((slots * 256, chans), jnp.float32)
    for index in range(27):
        field = field + jnp.dot(
            tap_slice(tiles, index, False), conv_weight[index], preferred_element_type=jnp.float32
        )
    field = field.reshape(slots, 256, chans) * livef
    active = jax.nn.silu(field)
    pooled = active.reshape(slots, 4, 2, 4, 2, 4, chans).mean(axis=(1, 3, 5))
    coarse_in = (
        jnp.einsum("kg,kyxc->ygxc", select, pooled).astype(jnp.bfloat16).reshape(cells, chans)
    )
    grid_g = (
        jnp.dot(coarse_in, down_weight, preferred_element_type=jnp.float32)
        .astype(jnp.bfloat16)
        .reshape(1, 2, span, wide)
    )
    depth = depth_weight.astype(jnp.float32)
    framed_g = coarse_frame(grid_g)
    grid_v = grid_g.astype(jnp.float32) + coarse_spread(framed_g, depth, False, span)
    grid_q = jax.nn.silu(grid_v).astype(jnp.bfloat16).reshape(cells, wide)
    upstream = cotangent[0, 0].astype(jnp.float32) * livef
    cell_sums = upstream.reshape(slots, 4, 2, 4, 2, 4, chans).sum(axis=(1, 3, 5))
    grad_z = (
        jnp.einsum("kg,kyxc->ygxc", select, cell_sums).astype(jnp.bfloat16).reshape(cells, chans)
    )
    up_part = lax.dot_general(
        grid_q, grad_z, (((0,), (0,)), ((), ())), preferred_element_type=jnp.float32
    )
    grad_q = lax.dot_general(
        grad_z, up_weight, (((1,), (1,)), ((), ())), preferred_element_type=jnp.float32
    )
    grad_v = (
        (grad_q * silu_slope(grid_v.reshape(cells, wide)))
        .astype(jnp.bfloat16)
        .reshape(1, 2, span, wide)
    )
    framed_v = coarse_frame(grad_v)
    grad_g = (grad_v.astype(jnp.float32) + coarse_spread(framed_v, depth, True, span)).astype(
        jnp.bfloat16
    )
    grad_vf = grad_v.astype(jnp.float32)
    terms = []
    for index in range(27):
        start_z, start_y, start_x = (index // 9, index // 3 % 3, index % 3)
        shifted = framed_g[
            start_z : start_z + 1, start_y : start_y + 2, start_x : start_x + span
        ].astype(jnp.float32)
        terms.append(jnp.sum(shifted * grad_vf, axis=(0, 1, 2)))
    depth_part = jnp.stack(terms, axis=0)
    grad_rows = grad_g.reshape(cells, wide)
    down_part = lax.dot_general(
        coarse_in, grad_rows, (((0,), (0,)), ((), ())), preferred_element_type=jnp.float32
    )
    down_grad, depth_grad, up_grad = lax.psum(
        (down_part, depth_part, up_part), ("blk", "slab", "ch")
    )
    grad_p = lax.dot_general(
        grad_rows, down_weight, (((1,), (1,)), ((), ())), preferred_element_type=jnp.float32
    )
    grad_p_slots = jnp.einsum("kg,ygxc->kyxc", select, grad_p.reshape(2, GX, 2, chans))
    spread_p = jnp.broadcast_to(
        grad_p_slots.reshape(slots, 1, 2, 1, 2, 1, chans), (slots, 4, 2, 4, 2, 4, chans)
    ).reshape(slots, 256, chans)
    grad_f = ((upstream + spread_p / 64.0) * silu_slope(field) * livef).astype(jnp.bfloat16)
    grad_tiles = fine_tiles(grad_f.reshape(slots, 4, 8, 8, chans), place)
    grad_flat = grad_f.reshape(slots * 256, chans)
    grad_inputs = jnp.zeros((slots * 256, chans), jnp.float32)
    weight_terms = []
    for index in range(27):
        grad_inputs = grad_inputs + lax.dot_general(
            tap_slice(grad_tiles, index, True),
            conv_weight[index],
            (((1,), (1,)), ((), ())),
            preferred_element_type=jnp.float32,
        )
        weight_terms.append(
            lax.dot_general(
                tap_slice(tiles, index, False),
                grad_flat,
                (((0,), (0,)), ((), ())),
                preferred_element_type=jnp.float32,
            ).reshape(chans * chans)
        )
    weight_sum = jnp.stack(weight_terms, axis=0)
    input_grad = (
        (grad_inputs.reshape(slots, 256, chans) * livef)
        .astype(jnp.bfloat16)
        .reshape(1, 1, slots, 256, chans)
    )
    conv_grad = lax.psum_scatter(weight_sum, ("blk", "slab", "ch"), scatter_dimension=1, tiled=True)
    return (input_grad, conv_grad, down_grad, depth_grad, up_grad)


def solution(mesh):
    in_specs = (
        P(("groups", "slab", "ch"), "blk", None, None, None),
        P(("groups", "slab", "ch"), "blk", None, None, None),
        P(),
        P(),
        P(),
        P(),
        P(("groups", "slab", "ch"), "blk", None),
        P(("groups", "slab", "ch"), "blk", None, None),
    )
    out_specs = (
        P(("groups", "slab", "ch"), "blk", None, None, None),
        P("groups", ("blk", "slab", "ch")),
        P("groups", None),
        P("groups", None),
        P("groups", None),
    )
    return jax.shard_map(
        per_device, mesh=mesh, in_specs=in_specs, out_specs=out_specs, check_vma=False
    )
```

profile of v0, /device:TPU:0, one launch (start us, length us, event | category | flops | bytes accessed | tf_op | source)
XLA Modules:
  0.0 355.0 jit_solution(3404647641314009250)
XLA Ops:
  10.2 4.9 %collective-permute-start = (bf16[4,1,96,128]{3,1,0,2:T(2,128)(2,1)S(1)}, bf16[4,1,96,128]{3,1,0,2:T(2,128)(2,1)S(1)}, u32[]{:S(2)}, u32[]{:S(2)}) collective-permute-start(bf16[4,1,96,128]{3,1,0,2:T(2,128)(2,1)S(1)} %get-tuple-element.102), channel_id=1, source_target_pairs={{0,4},{4,8},{8,12},{1,5},{5,9},{9,13},{2,6},{6,10},{10,14},{3,7},{... | collective-permute-start | bytes 294920 | tf_op jit(solution)/shard_map/ppermute | solution.py:16
  17.1 2.2 collective-permute-done
  19.3 4.1 %collective-permute-done.1 = bf16[4,1,96,128]{3,1,0,2:T(2,128)(2,1)S(1)} collective-permute-done((bf16[4,1,96,128]{3,1,0,2:T(2,128)(2,1)S(1)}, bf16[4,1,96,128]{3,1,0,2:T(2,128)(2,1)S(1)}, u32[]{:S(2)}, u32[]{:S(2)}) %collective-permute-start.1) | collective-permute-done | bytes 98336 | tf_op jit(solution)/shard_map/ppermute | solution.py:17
  28.0 2.5 collective-permute-done.3
  30.5 2.6 fusion.10
  46.3 3.5 collective-permute-start.4
  49.7 1.5 collective-permute-start.5
  51.3 4.2 %collective-permute-done.5 = bf16[1,1,24,256]{3,2,1,0:T(8,128)(2,1)S(1)} collective-permute-done((bf16[1,1,24,256]{3,2,1,0:T(8,128)(2,1)S(1)}, bf16[1,1,24,256]{3,2,1,0:T(8,128)(2,1)S(1)}, u32[]{:S(2)}, u32[]{:S(2)}) %collective-permute-start.5) | collective-permute-done | bytes 12320 | tf_op jit(solution)/shard_map/ppermute | solution.py:17
  56.8 7.1 %collective-permute-start.6 = (bf16[1,4,24,256]{3,2,1,0:T(8,128)(2,1)S(1)}, bf16[1,4,24,256]{3,2,1,0:T(8,128)(2,1)S(1)}, u32[]{:S(2)}, u32[]{:S(2)}) collective-permute-start(bf16[1,4,24,256]{3,2,1,0:T(8,128)(2,1)S(1)} %pad_maximum_fusion.6), channel_id=1, source_target_pairs={{0,1},{1,2},{2,3},{4,5},{5,6},{6,7},{8,9},{9,10},{10,11},{12,13},{... | collective-permute-start | bytes 147464 | tf_op jit(solution)/shard_map/ppermute | solution.py:16
  66.1 3.5 collective-permute-start.8
  72.4 2.7 collective-permute-done.9
  77.1 3.1 collective-permute-start.10
  80.8 2.8 stack.115
  83.7 61.9 %psum.22 = f32[27,256]{1,0:T(8,128)} all-reduce(f32[27,256]{1,0:T(8,128)S(1)} %stack.115), channel_id=1, replica_groups=mesh['groups'=2,'blk'=4,'slab'=2,'ch'=2] {'blk','slab','ch'}, use_global_device_ids=true, to_apply=%region_31.32 | all-reduce | flops 6912 | bytes 55296 | tf_op jit(solution)/shard_map/psum | solution.py:139
  151.6 1.9 fusion.274
  153.5 1.9 fusion.273
  155.4 1.9 fusion.272
  181.4 4.4 %collective-permute-done.13 = bf16[4,1,96,128]{3,1,0,2:T(2,128)(2,1)S(1)} collective-permute-done((bf16[4,1,96,128]{3,1,0,2:T(2,128)(2,1)S(1)}, bf16[4,1,96,128]{3,1,0,2:T(2,128)(2,1)S(1)}, u32[]{:S(2)}, u32[]{:S(2)}) %collective-permute-start.13) | collective-permute-done | bytes 98336 | tf_op jit(solution)/shard_map/ppermute | solution.py:17
  191.8 7.1 %stack.87 = f32[27,16384]{1,0:T(8,128)} concatenate(f32[1,16384]{1,0:T(1,128)} %bitcast.602, f32[1,16384]{1,0:T(1,128)} %bitcast.601, f32[1,16384]{1,0:T(1,128)} %bitcast.600, f32[1,16384]{1,0:T(1,128)} %bitcast.599, f32[1,16384]{1,0:T(1,128)} %bitcast.598, f32[1,16384]{1,0:T(1,128)} %bitcast.597, f32[1,16384]{1,0:T(1,128)} %bitcast.596, f32[1,16384]{1,0:T(1,128)} %bitcast.595, ...), dimensions={0} | concatenate | bytes 3538944 | tf_op jit(solution)/shard_map/stack | solution.py:169
  199.7 3.7 %select_maximum_fusion = bf16[6,10,98,128]{3,1,0,2:T(8,128)(2,1)S(1)} fusion(bf16[1,10,96,128]{3,1,0,2:T(8,128)(2,1)} %collective-permute-done.15, bf16[1,10,96,128]{3,1,0,2:T(8,128)(2,1)} %copy-done.42, bf16[4,1,96,128]{3,1,0,2:T(2,128)(2,1)S(1)} %copy-done.41, bf16[4,8,96,128]{3,1,0,2:T(8,128)(2,1)S(1)} %bitcast.473, bf16[4,1,96,128]{3,1,0,2:T(2,128)(2,1)} %copy-done.39), kind=kLoop, calls=%fused_computation.5 | loop fusion | flops 13547520 | bytes 2979840 | tf_op jit(solution)/shard_map/concatenate | solution.py:18
  215.9 62.8 %all-reduce.7.cloned.1.call-done = (f32[128,256]{1,0:T(8,128)}, f32[256,128]{1,0:T(8,128)}) async-done(((f32[128,256]{1,0:T(8,128)}, f32[256,128]{1,0:T(8,128)}), (f32[128,256]{1,0:T(8,128)}, f32[256,128]{1,0:T(8,128)})) %all-reduce.7.cloned.1.call-update) | async-done | bytes 262160 | tf_op jit(solution)/shard_map/psum | solution.py:139
  278.7 66.4 %reduce-scatter.2.cloned.1.call-done = f32[27,1024]{1,0:T(8,128)} async-done(((f32[27,16384]{1,0:T(8,128)}), f32[27,1024]{1,0:T(8,128)}) %reduce-scatter.2.cloned.1.call-update) | async-done | bytes 110608 | tf_op jit(solution)/shard_map/reduce_scatter | solution.py:175
  345.1 1.6 copy.405
  346.6 1.6 copy.406
  (389 shorter events, 79.1 us)
Async XLA Ops:
  7.2 271.5 %all-reduce.7.cloned.1.call-start = ((), (), s32[]{:S(2)}) async-start(), calls=%async_computation.2 | async-start | bytes 524288 | tf_op jit(solution)/shard_map/psum | solution.py:139
  10.2 9.1 %collective-permute-start = (bf16[4,1,96,128]{3,1,0,2:T(2,128)(2,1)S(1)}, bf16[4,1,96,128]{3,1,0,2:T(2,128)(2,1)S(1)}, u32[]{:S(2)}, u32[]{:S(2)}) collective-permute-start(bf16[4,1,96,128]{3,1,0,2:T(2,128)(2,1)S(1)} %get-tuple-element.102), channel_id=1, source_target_pairs={{0,4},{4,8},{8,12},{1,5},{5,9},{9,13},{2,6},{6,10},{10,14},{3,7},{... | collective-permute-start | bytes 294920 | tf_op jit(solution)/shard_map/ppermute | solution.py:16
  15.1 8.3 %collective-permute-start.1 = (bf16[4,1,96,128]{3,1,0,2:T(2,128)(2,1)S(1)}, bf16[4,1,96,128]{3,1,0,2:T(2,128)(2,1)S(1)}, u32[]{:S(2)}, u32[]{:S(2)}) collective-permute-start(bf16[4,1,96,128]{3,1,0,2:T(2,128)(2,1)S(1)} %get-tuple-element.103), channel_id=1, source_target_pairs={{4,0},{8,4},{12,8},{5,1},{9,5},{13,9},{6,2},{10,6},{14,10},{7,3},{... | collective-permute-start | bytes 294920 | tf_op jit(solution)/shard_map/ppermute | solution.py:17
  17.1 34.1 %copy-start.86 = (f32[4]{0:T(128)}, f32[4]{0:T(128)S(1)}, u32[]{:S(2)}) copy-start(f32[4]{0:T(128)S(1)} %compare_convert_fusion) | copy-start | bytes 52
  23.9 4.1 %collective-permute-start.2 = (bf16[1,10,96,128]{3,1,0,2:T(8,128)(2,1)S(1)}, bf16[1,10,96,128]{3,1,0,2:T(8,128)(2,1)S(1)}, u32[]{:S(2)}, u32[]{:S(2)}) collective-permute-start(bf16[1,10,96,128]{3,1,0,2:T(8,128)(2,1)S(1)} %get-tuple-element.44), channel_id=1, source_target_pairs={{0,1},{1,2},{2,3},{4,5},{5,6},{6,7},{8,9},{9,10},{10,11},{12,13},{... | collective-permute-start | bytes 737288 | tf_op jit(solution)/shard_map/ppermute | solution.py:16
  25.2 5.3 %collective-permute-start.3 = (bf16[1,10,96,128]{3,1,0,2:T(8,128)(2,1)S(1)}, bf16[1,10,96,128]{3,1,0,2:T(8,128)(2,1)S(1)}, u32[]{:S(2)}, u32[]{:S(2)}) collective-permute-start(bf16[1,10,96,128]{3,1,0,2:T(8,128)(2,1)S(1)} %get-tuple-element.45), channel_id=1, source_target_pairs={{1,0},{2,1},{3,2},{5,4},{6,5},{7,6},{9,8},{10,9},{11,10},{13,12},{... | collective-permute-start | bytes 737288 | tf_op jit(solution)/shard_map/ppermute | solution.py:17
  44.6 20.2 %copy-start.59 = (f32[1,256]{1,0:T(1,128)S(1)}, f32[1,256]{1,0:T(1,128)}, u32[]{:S(2)}) copy-start(f32[1,256]{1,0:T(1,128)} %get-tuple-element.127) | copy-start | bytes 3076
  44.6 20.2 %copy-start.60 = (f32[1,256]{1,0:T(1,128)S(1)}, f32[1,256]{1,0:T(1,128)}, u32[]{:S(2)}) copy-start(f32[1,256]{1,0:T(1,128)} %get-tuple-element.128) | copy-start | bytes 3076
  44.6 20.2 %copy-start.61 = (f32[1,256]{1,0:T(1,128)S(1)}, f32[1,256]{1,0:T(1,128)}, u32[]{:S(2)}) copy-start(f32[1,256]{1,0:T(1,128)} %get-tuple-element.129) | copy-start | bytes 3076
  45.1 20.2 %copy-start.57 = (bf16[256,128]{1,0:T(8,128)(2,1)S(1)}, bf16[256,128]{1,0:T(8,128)(2,1)}, u32[]{:S(2)}) copy-start(bf16[256,128]{1,0:T(8,128)(2,1)} %param.13) | copy-start | bytes 196612
  46.3 5.0 %collective-permute-start.4 = (bf16[1,1,24,256]{3,2,1,0:T(8,128)(2,1)S(1)}, bf16[1,1,24,256]{3,2,1,0:T(8,128)(2,1)S(1)}, u32[]{:S(2)}, u32[]{:S(2)}) collective-permute-start(bf16[1,1,24,256]{3,2,1,0:T(8,128)(2,1)S(1)} %get-tuple-element.106), channel_id=1, source_target_pairs={{0,4},{4,8},{8,12},{1,5},{5,9},{9,13},{2,6},{6,10},{10,14},{3,7},{... | collective-permute-start | bytes 36872 | tf_op jit(solution)/shard_map/ppermute | solution.py:16
  49.7 5.8 %collective-permute-start.5 = (bf16[1,1,24,256]{3,2,1,0:T(8,128)(2,1)S(1)}, bf16[1,1,24,256]{3,2,1,0:T(8,128)(2,1)S(1)}, u32[]{:S(2)}, u32[]{:S(2)}) collective-permute-start(bf16[1,1,24,256]{3,2,1,0:T(8,128)(2,1)S(1)} %get-tuple-element.107), channel_id=1, source_target_pairs={{4,0},{8,4},{12,8},{5,1},{9,5},{13,9},{6,2},{10,6},{14,10},{7,3},{... | collective-permute-start | bytes 36872 | tf_op jit(solution)/shard_map/ppermute | solution.py:17
  55.5 8.7 %collective-permute-start.7 = (bf16[1,4,24,256]{3,2,1,0:T(8,128)(2,1)S(1)}, bf16[1,4,24,256]{3,2,1,0:T(8,128)(2,1)S(1)}, u32[]{:S(2)}, u32[]{:S(2)}) collective-permute-start(bf16[1,4,24,256]{3,2,1,0:T(8,128)(2,1)S(1)} %pad_maximum_fusion.6), channel_id=1, source_target_pairs={{1,0},{2,1},{3,2},{5,4},{6,5},{7,6},{9,8},{10,9},{11,10},{13,12},{... | collective-permute-start | bytes 147464 | tf_op jit(solution)/shard_map/ppermute | solution.py:17
  56.8 8.0 %collective-permute-start.6 = (bf16[1,4,24,256]{3,2,1,0:T(8,128)(2,1)S(1)}, bf16[1,4,24,256]{3,2,1,0:T(8,128)(2,1)S(1)}, u32[]{:S(2)}, u32[]{:S(2)}) collective-permute-start(bf16[1,4,24,256]{3,2,1,0:T(8,128)(2,1)S(1)} %pad_maximum_fusion.6), channel_id=1, source_target_pairs={{0,1},{1,2},{2,3},{4,5},{5,6},{6,7},{8,9},{9,10},{10,11},{12,13},{... | collective-permute-start | bytes 147464 | tf_op jit(solution)/shard_map/ppermute | solution.py:16
  66.1 6.4 %collective-permute-start.8 = (bf16[1,1,24,256]{3,2,1,0:T(8,128)(2,1)S(1)}, bf16[1,1,24,256]{3,2,1,0:T(8,128)(2,1)S(1)}, u32[]{:S(2)}, u32[]{:S(2)}) collective-permute-start(bf16[1,1,24,256]{3,2,1,0:T(8,128)(2,1)S(1)} %get-tuple-element.104), channel_id=1, source_target_pairs={{0,4},{4,8},{8,12},{1,5},{5,9},{9,13},{2,6},{6,10},{10,14},{3,7},{... | collective-permute-start | bytes 36872 | tf_op jit(solution)/shard_map/ppermute | solution.py:16
  69.6 5.6 %collective-permute-start.9 = (bf16[1,1,24,256]{3,2,1,0:T(8,128)(2,1)S(1)}, bf16[1,1,24,256]{3,2,1,0:T(8,128)(2,1)S(1)}, u32[]{:S(2)}, u32[]{:S(2)}) collective-permute-start(bf16[1,1,24,256]{3,2,1,0:T(8,128)(2,1)S(1)} %get-tuple-element.105), channel_id=1, source_target_pairs={{4,0},{8,4},{12,8},{5,1},{9,5},{13,9},{6,2},{10,6},{14,10},{7,3},{... | collective-permute-start | bytes 36872 | tf_op jit(solution)/shard_map/ppermute | solution.py:17
  75.8 69.8 %collective-permute-start.11 = (bf16[1,4,24,256]{3,2,1,0:T(8,128)(2,1)}, bf16[1,4,24,256]{3,2,1,0:T(8,128)(2,1)S(1)}, u32[]{:S(2)}, u32[]{:S(2)}) collective-permute-start(bf16[1,4,24,256]{3,2,1,0:T(8,128)(2,1)} %pad_maximum_fusion.7), channel_id=1, source_target_pairs={{1,0},{2,1},{3,2},{5,4},{6,5},{7,6},{9,8},{10,9},{11,10},{13,12},{... | collective-permute-start | bytes 147464 | tf_op jit(solution)/shard_map/ppermute | solution.py:17
  77.1 68.5 %collective-permute-start.10 = (bf16[1,4,24,256]{3,2,1,0:T(8,128)(2,1)}, bf16[1,4,24,256]{3,2,1,0:T(8,128)(2,1)S(1)}, u32[]{:S(2)}, u32[]{:S(2)}) collective-permute-start(bf16[1,4,24,256]{3,2,1,0:T(8,128)(2,1)} %pad_maximum_fusion.7), channel_id=1, source_target_pairs={{0,1},{1,2},{2,3},{4,5},{5,6},{6,7},{8,9},{9,10},{10,11},{12,13},{... | collective-permute-start | bytes 147464 | tf_op jit(solution)/shard_map/ppermute | solution.py:16
  177.0 4.5 %collective-permute-start.12 = (bf16[4,1,96,128]{3,1,0,2:T(2,128)(2,1)S(1)}, bf16[4,1,96,128]{3,1,0,2:T(2,128)(2,1)S(1)}, u32[]{:S(2)}, u32[]{:S(2)}) collective-permute-start(bf16[4,1,96,128]{3,1,0,2:T(2,128)(2,1)S(1)} %get-tuple-element.100), channel_id=1, source_target_pairs={{0,4},{4,8},{8,12},{1,5},{5,9},{9,13},{2,6},{6,10},{10,14},{3,7},{... | collective-permute-start | bytes 294920 | tf_op jit(solution)/shard_map/ppermute | solution.py:16
  178.3 7.6 %collective-permute-start.13 = (bf16[4,1,96,128]{3,1,0,2:T(2,128)(2,1)S(1)}, bf16[4,1,96,128]{3,1,0,2:T(2,128)(2,1)S(1)}, u32[]{:S(2)}, u32[]{:S(2)}) collective-permute-start(bf16[4,1,96,128]{3,1,0,2:T(2,128)(2,1)S(1)} %get-tuple-element.101), channel_id=1, source_target_pairs={{4,0},{8,4},{12,8},{5,1},{9,5},{13,9},{6,2},{10,6},{14,10},{7,3},{... | collective-permute-start | bytes 294920 | tf_op jit(solution)/shard_map/ppermute | solution.py:17
  187.0 11.9 %collective-permute-start.14 = (bf16[1,10,96,128]{3,1,0,2:T(8,128)(2,1)S(1)}, bf16[1,10,96,128]{3,1,0,2:T(8,128)(2,1)S(1)}, u32[]{:S(2)}, u32[]{:S(2)}) collective-permute-start(bf16[1,10,96,128]{3,1,0,2:T(8,128)(2,1)S(1)} %get-tuple-element.42), channel_id=1, source_target_pairs={{0,1},{1,2},{2,3},{4,5},{5,6},{6,7},{8,9},{9,10},{10,11},{12,13},{... | collective-permute-start | bytes 737288 | tf_op jit(solution)/shard_map/ppermute | solution.py:16
  188.3 11.4 %collective-permute-start.15 = (bf16[1,10,96,128]{3,1,0,2:T(8,128)(2,1)S(1)}, bf16[1,10,96,128]{3,1,0,2:T(8,128)(2,1)}, u32[]{:S(2)}, u32[]{:S(2)}) collective-permute-start(bf16[1,10,96,128]{3,1,0,2:T(8,128)(2,1)S(1)} %get-tuple-element.43), channel_id=1, source_target_pairs={{1,0},{2,1},{3,2},{5,4},{6,5},{7,6},{9,8},{10,9},{11,10},{13,12},{... | collective-permute-start | bytes 737288 | tf_op jit(solution)/shard_map/ppermute | solution.py:17
  190.5 154.6 %reduce-scatter.2.cloned.1.call-start = ((), (), s32[]{:S(2)}) async-start(), calls=%async_computation.1 | async-start | bytes 2228224 | tf_op jit(solution)/shard_map/reduce_scatter | solution.py:175
  214.4 133.8 %copy-start.1 = (bf16[1,1,4,256,128]{4,3,2,1,0:T(8,128)(2,1)S(1)}, bf16[1,1,4,256,128]{4,3,2,1,0:T(8,128)(2,1)}, u32[]{:S(2)}) copy-start(bf16[1,1,4,256,128]{4,3,2,1,0:T(8,128)(2,1)} %param.8) | copy-start | bytes 786436
  (86 other events, 996.3 us)
Sparse Core Ops, SparseCore 0:
  190.6 88.0 all-reduce.6
  283.0 62.0 reduce-scatter.1
where the time goes:
time: 356 us; the launch traced here: 355 us
  waiting for transfers between devices  151 us (42%)
  blocking collectives  61.9 us (17%)
  matrix products  45.4 us (13%)
  starting transfers between devices  36.8 us (10%)
  local copies, waits for them, and re-layouts  29.6 us (8%)
  between operations  16.2 us (5%)
  other arithmetic  14.3 us (4%)
    reduce_scatter x1, waiting for transfers between devices, per_device(): lax.psum_scatter(weight_sum, ('blk', 'slab', 'ch'), scatter_dimension=1,...  66.4 us
    psum x1, waiting for transfers between devices, per_device(): lax.psum((down_part, depth_part, up_part), ('blk', 'slab', 'ch'))  62.8 us
    psum x1, blocking collectives, per_device(): lax.psum((down_part, depth_part, up_part), ('blk', 'slab', 'ch'))  61.9 us
    dot_general x27, matrix products, per_device(): lax.dot_general(tap_slice(tiles, index, False), grad_flat, (((0,), (0,)),...  27.8 us
    ppermute x8, starting transfers between devices, with_halo(): before = lax.ppermute(last, axis, up)  26 us
    ppermute x8, waiting for transfers between devices, with_halo(): after = lax.ppermute(leading, axis, down)  17.9 us
    ppermute x8, starting transfers between devices, with_halo(): after = lax.ppermute(leading, axis, down)  10.5 us
    slice x58, local copies, waits for them, and re-layouts, tap_slice(): tiles[:, start_z:start_z + 4, start_y:start_y + 8, start_x:start_x + 8]  8.29 us
  transfers between devices with their start and end apart: 18, of which 10 were waited for; matrix products, arithmetic and copies ran while one was open for 9% of the time, Pallas kernels for 0%

commit v1 on v0

v1 whole, which is shorter than its diff:
```python
import functools

import jax
import jax.numpy as jnp
import numpy as np
from jax import lax
from jax.experimental import pallas as pl
from jax.experimental.pallas import tpu as pltpu
from jax.sharding import PartitionSpec as P

F32 = jnp.float32
BF16 = jnp.bfloat16
HIGH = lax.Precision.HIGHEST
DIRS = [(da, db) for da in (-1, 0, 1) for db in (-1, 0, 1) if (da, db) != (0, 0)]


def silu_slope(value):
    sigma = jax.nn.sigmoid(value)
    return sigma * (1.0 + value * (1.0 - sigma))


def level_kernel(
    sizes, reduce, nb, x_in, cot_in, conv_w, down_w, depth_w, up_w, idx_in,
    dx_out, cw_out, dn_out, dp_out, up_out,
    C0, NZ, NY, NC, hz, hy, hc, sz, sy, sc, FR, T, FS, DF, WB, GA, WF,
    st1, rv1, st2, rv2, sms, smr, ag, DG,
    hs, hr, cs, cr, p1s, p1r, p2s, p2r, ss, sr, gs, gr,
):
    B, S, H = sizes
    K = 4
    blk, slab, ch = lax.axis_index("blk"), lax.axis_index("slab"), lax.axis_index("ch")
    row = slab * H + ch
    rows = S * H
    n = B * S * H
    me = blk * rows + row

    def target(d):
        return {"blk": lax.div(d, rows), "slab": lax.rem(lax.div(d, H), S), "ch": lax.rem(d, H)}

    def exists(da, db):
        r, c = row + da, blk + db
        return (r >= 0) & (r < rows) & (c >= 0) & (c < B)

    def beside(da, db):
        return target((blk + db) * rows + row + da)

    for ref in (hz, hy, hc, GA, sms):
        ref[...] = jnp.zeros(ref.shape, ref.dtype)
    C0[K] = jnp.zeros(C0.shape[1:], F32)
    NZ[:, K] = jnp.zeros((2,) + NZ.shape[2:], F32)
    NY[:, K] = jnp.zeros((2,) + NY.shape[2:], F32)
    NC[:, K] = jnp.zeros((4,) + NC.shape[2:], F32)
    barrier = pltpu.get_barrier_semaphore()
    if reduce:
        def greet(r, carry):
            pl.semaphore_signal(barrier, inc=1, device_id=target(lax.rem(me + r, n)),
                                device_id_type=pl.DeviceIdType.MESH)
            return carry
        lax.fori_loop(1, n, greet, 0)
    else:
        for da, db in DIRS:
            @pl.when(exists(da, db))
            def _():
                pl.semaphore_signal(barrier, inc=1, device_id=beside(da, db),
                                    device_id_type=pl.DeviceIdType.MESH)

    def entered():
        if reduce:
            pl.semaphore_wait(barrier, n - 1)
        else:
            for da, db in DIRS:
                @pl.when(exists(da, db))
                def _():
                    pl.semaphore_wait(barrier, 1)

    def copy(src, dst, s, r, dev):
        return pltpu.make_async_remote_copy(
            src_ref=src, dst_ref=dst, send_sem=s, recv_sem=r, device_id=dev,
            device_id_type=pl.DeviceIdType.MESH)

    def face(ph, i, send):
        da, db = DIRS[i]
        if db == 0:
            return (sz if send else hz).at[ph, int(da > 0)]
        if da == 0:
            return (sy if send else hy).at[ph, int(db > 0)]
        return (sc if send else hc).at[ph, 2 * int(da > 0) + int(db > 0)]

    def stage(ph):
        for s in (0, 1):
            sz[ph, s] = C0[0:K, 3 * s].reshape(K * 64, 128).astype(BF16)
            sy[ph, s] = C0[0:K, :, 7 * s].reshape(K * 32, 128).astype(BF16)
            for u in (0, 1):
                sc[ph, 2 * s + u] = C0[0:K, 3 * s, 7 * u].reshape(K * 8, 128).astype(BF16)

    def send_halo(ph):
        for i, (da, db) in enumerate(DIRS):
            @pl.when(exists(da, db))
            def _():
                copy(face(ph, i, True), face(ph, 7 - i, False), hs.at[ph, i], hr.at[ph, 7 - i],
                     beside(da, db)).start()

    def wait_halo(ph):
        for i, (da, db) in enumerate(DIRS):
            @pl.when(exists(da, db))
            def _():
                copy(face(ph, i, True), face(ph, i, False), hs.at[ph, i], hr.at[ph, i],
                     beside(da, db)).wait()
        NZ[:, 0:K] = hz[ph].astype(F32).reshape(2, K, 8, 8, 128)
        NY[:, 0:K] = hy[ph].astype(F32).reshape(2, K, 4, 8, 128)
        NC[:, 0:K] = hc[ph].astype(F32).reshape(4, K, 8, 128)

    def send_coarse(ph):
        for i, (da, db) in enumerate(DIRS):
            @pl.when(exists(da, db))
            def _():
                copy(GA.at[ph, 4], GA.at[ph, 4 - 3 * da - db], cs.at[ph, i], cr.at[ph, 7 - i],
                     beside(da, db)).start()

    def wait_coarse(ph):
        for i, (da, db) in enumerate(DIRS):
            @pl.when(exists(da, db))
            def _():
                copy(GA.at[ph, 4], GA.at[ph, 4 + 3 * da + db], cs.at[ph, i], cr.at[ph, i],
                     beside(da, db)).wait()

    def build():
        xi = lax.broadcasted_iota(jnp.int32, (60, 8, 128), 1)

        def slot(k, carry):
            for e in range(3):
                def at(a, b):
                    v = nb[k, 9 * a + 3 * b + e]
                    return jnp.where(v < 0, K, v)
                FR[e, 1:5, 1:9] = C0[at(1, 1)]
                FR[e, 1:5, 0] = NY[0, at(1, 0)]
                FR[e, 1:5, 9] = NY[1, at(1, 2)]
                FR[e, 0, 1:9] = NZ[0, at(0, 1)]
                FR[e, 5, 1:9] = NZ[1, at(2, 1)]
                FR[e, 0, 0] = NC[0, at(0, 0)]
                FR[e, 0, 9] = NC[1, at(0, 2)]
                FR[e, 5, 0] = NC[2, at(2, 0)]
                FR[e, 5, 9] = NC[3, at(2, 2)]
            mid = FR[1].reshape(60, 8, 128)
            first = pltpu.roll(jnp.where(xi == 7, FR[0].reshape(60, 8, 128), mid), 1, 1)
            last = pltpu.roll(jnp.where(xi == 0, FR[2].reshape(60, 8, 128), mid), 7, 1)
            for e, part in enumerate((first, mid, last)):
                part = part.reshape(6, 10, 8, 128)
                for b in range(3):
                    t = 3 * b + e
                    T[:, k, :, 128 * t:128 * t + 128] = (
                        part[:, b:b + 8].reshape(6, 64, 128).astype(BF16))
            return carry

        lax.fori_loop(0, K, slot, 0)

    C0[0:K] = x_in[...].astype(F32).reshape(K, 4, 8, 8, 128)
    stage(0)
    entered()
    send_halo(0)

    for a in range(3):
        for t in range(9):
            WB[a, 128 * t:128 * t + 128, :] = conv_w[26 - 9 * a - t].astype(F32).T.astype(BF16)
    live = [jnp.where(nb[k, 13] >= 0, 1.0, 0.0).astype(F32) for k in range(K)]
    r_i = lax.broadcasted_iota(jnp.int32, (16, 64), 0)
    c_i = lax.broadcasted_iota(jnp.int32, (16, 64), 1)
    pool = ((r_i // 2 == c_i // 8) & (r_i % 2 == (c_i % 8) // 4)).astype(F32)
    r_j = lax.broadcasted_iota(jnp.int32, (64, 16), 1)
    c_j = lax.broadcasted_iota(jnp.int32, (64, 16), 0)
    unpool = ((r_j // 2 == c_j // 8) & (r_j % 2 == (c_j % 8) // 4)).astype(F32)
    cot_rows = jnp.concatenate(
        [cot_in[k].astype(F32).reshape(4, 2, 4, 8, 128).sum(axis=(0, 2)) * live[k]
         for k in range(K)], axis=0).reshape(64, 128)
    dz = jnp.dot(pool, cot_rows, precision=HIGH, preferred_element_type=F32).astype(BF16)
    grad_q = lax.dot_general(dz, up_w[...], (((1,), (1,)), ((), ())), preferred_element_type=F32)
    pick = (idx_in[...] == lax.broadcasted_iota(jnp.int32, (432, 144), 1)).astype(F32).astype(BF16)
    depth = depth_w[...].astype(F32)
    WF[:, 9] = jnp.zeros((3, 128, 128), F32)

    wait_halo(0)
    build()
    for a in range(3):
        term = jnp.dot(T[a:a + 4].reshape(1024, 1152), conv_w[9 * a:9 * a + 9].reshape(1152, 128),
                       preferred_element_type=F32).reshape(4, K, 64, 128)
        if a == 0:
            FS[...] = term
        else:
            FS[...] += term
    field = FS[...]
    act = field * jax.nn.sigmoid(field)
    act_rows = act.sum(axis=0).reshape(K, 2, 4, 8, 128).sum(axis=2).reshape(64, 128)
    p = jnp.dot(pool, act_rows * (1.0 / 64.0), precision=HIGH, preferred_element_type=F32)
    p = p.astype(BF16)
    g = jnp.dot(p, down_w[...], preferred_element_type=F32).astype(BF16)
    GA[0, 4] = g
    send_coarse(0)
    wait_coarse(0)
    near = jnp.dot(pick, GA[0].reshape(144, 256), preferred_element_type=F32)
    v = jnp.zeros((16, 256), F32)
    for t in range(27):
        v = v + near[16 * t:16 * t + 16] * depth[t:t + 1]
    v = v + g.astype(F32)
    dv = (grad_q * silu_slope(v)).astype(BF16)
    GA[1, 4] = dv
    send_coarse(1)
    dvf = dv.astype(F32)
    q = (v * jax.nn.sigmoid(v)).astype(BF16)
    up_part = lax.dot_general(q, dz, (((0,), (0,)), ((), ())), preferred_element_type=F32)
    DG[...] = jnp.zeros(DG.shape, F32)
    for t in range(27):
        line = jnp.sum(near[16 * t:16 * t + 16] * dvf, axis=0, keepdims=True)
        DG[t:t + 1] = line[:, :128]
        DG[32 + t:33 + t] = line[:, 128:]
    wait_coarse(1)
    near = jnp.dot(pick, GA[1].reshape(144, 256), preferred_element_type=F32)
    dg = jnp.zeros((16, 256), F32)
    for t in range(27):
        u = 26 - t
        dg = dg + near[16 * u:16 * u + 16] * depth[t:t + 1]
    dg = (dg + dvf).astype(BF16)
    dp = lax.dot_general(dg, down_w[...], (((1,), (1,)), ((), ())), preferred_element_type=F32)
    wide = jnp.dot(unpool, dp * (1.0 / 64.0), precision=HIGH, preferred_element_type=F32)
    wide = wide.reshape(K, 2, 8, 128)
    for k in range(K):
        up_rows = cot_in[k].astype(F32).reshape(4, 2, 4, 8, 128) + wide[k].reshape(1, 2, 1, 8, 128)
        slope = silu_slope(FS[:, k]).reshape(4, 2, 4, 8, 128)
        df = (up_rows * slope * live[k]).astype(BF16)
        DF[:, k] = df.reshape(4, 64, 128)
        C0[k] = df.astype(F32).reshape(4, 8, 8, 128)
    stage(1)
    send_halo(1)
    down_part = lax.dot_general(p, dg, (((0,), (0,)), ((), ())), preferred_element_type=F32)

    if reduce:
        sms[:, 0:16] = up_part.reshape(16, 16, 128).astype(BF16)
        sms[0:8, 16:32] = down_part[:, :128].reshape(8, 16, 128).astype(BF16)
        sms[8:16, 16:32] = down_part[:, 128:].reshape(8, 16, 128).astype(BF16)
        sms[0:4, 32:48] = DG[...].reshape(4, 16, 128).astype(BF16)

        def small(r):
            to = lax.rem(me + r, n)
            return copy(sms.at[to], smr.at[me], ss.at[r], sr.at[r], target(to))

        def small_in(r):
            src = lax.rem(me - r + n, n)
            return copy(sms.at[src], smr.at[src], ss.at[r], sr.at[r], target(src))

        def final(r):
            to = lax.rem(me + r, n)
            return copy(ag.at[me], ag.at[me], gs.at[r], gr.at[r], target(to))

        def final_in(r):
            src = lax.rem(me - r + n, n)
            return copy(ag.at[src], ag.at[src], gs.at[r], gr.at[r], target(src))

        def each(count, fn):
            def body(r, carry):
                fn(r)
                return carry
            lax.fori_loop(1, count, body, 0)

        each(n, lambda r: small(r).start())
    else:
        up_out[...] = up_part
        dn_out[...] = down_part
        dp_out[:, :128] = DG[0:27]
        dp_out[:, 128:] = DG[32:59]

    Q = B * S
    mine = blk * S + slab
    other = 1 - ch

    def pair(a):
        return copy(st1.at[a], rv1.at[a], p1s.at[a], p1r.at[a],
                    {"blk": blk, "slab": slab, "ch": other})

    def spread_to(a, r):
        to = lax.rem(mine + r, Q)
        return copy(st2.at[a, to], rv2.at[a, mine], p2s.at[a, r], p2r.at[a, r],
                    {"blk": lax.div(to, S), "slab": lax.rem(to, S), "ch": ch})

    def spread_in(a, r):
        src = lax.rem(mine - r + Q, Q)
        return copy(st2.at[a, src], rv2.at[a, src], p2s.at[a, r], p2r.at[a, r],
                    {"blk": lax.div(src, S), "slab": lax.rem(src, S), "ch": ch})

    def forward_pair(a):
        pair(a).wait()
        for qi in range(Q):
            at = pl.multiple_of(8 * (2 * qi + ch), 8)
            st2[a, qi] = (WF[a, :, pl.ds(at, 8)].reshape(80, 128)
                          + rv1[a, qi].astype(F32)).astype(BF16)
        each(Q, lambda r: spread_to(a, r).start())

    for a in range(3):
        wg = lax.dot_general(T[a:a + 4].reshape(1024, 1152), DF[...].reshape(1024, 128),
                             (((0,), (0,)), ((), ())), preferred_element_type=F32)
        WF[a, 0:9] = wg.reshape(9, 128, 128)
        if reduce:
            for qi in range(Q):
                at = pl.multiple_of(8 * (2 * qi + other), 8)
                st1[a, qi] = WF[a, :, pl.ds(at, 8)].reshape(80, 128).astype(BF16)
            pair(a).start()
            if a > 0:
                forward_pair(a - 1)
        else:
            cw_out[9 * a:9 * a + 9] = wg.reshape(9, 128, 128)
    if reduce:
        each(n, lambda r: small_in(r).wait())
        smr[me] = sms[me]
        total = smr[0].astype(F32)
        for d in range(1, 16):
            total = total + smr[d].astype(F32)
        ag[me] = total.astype(BF16)
        each(n, lambda r: final(r).start())
        forward_pair(2)

    wait_halo(1)
    build()
    for a in range(3):
        term = jnp.dot(T[a:a + 4].reshape(1024, 1152), WB[a],
                       preferred_element_type=F32).reshape(4, K, 64, 128)
        if a == 0:
            FS[...] = term
        else:
            FS[...] += term
    for k in range(K):
        dx_out[k] = FS[:, k].reshape(256, 128).astype(BF16)

    if reduce:
        each(n, lambda r: final_in(r).wait())
        up_out[...] = ag[:, 0:16].astype(F32).reshape(256, 128)
        dn_out[:, :128] = ag[0:8, 16:32].astype(F32).reshape(128, 128)
        dn_out[:, 128:] = ag[8:16, 16:32].astype(F32).reshape(128, 128)
        DG[...] = ag[0:4, 32:48].astype(F32).reshape(64, 128)
        dp_out[:, :128] = DG[0:27]
        dp_out[:, 128:] = DG[32:59]
        for a in range(3):
            each(Q, lambda r: spread_in(a, r).wait())
            rv2[a, mine] = st2[a, mine]
            total = rv2[a, 0].astype(F32)
            for qi in range(1, 8):
                total = total + rv2[a, qi].astype(F32)
            cw_out[9 * a:9 * a + 9] = total.reshape(10, 8, 128)[0:9]


def coarse_sources():
    block = np.zeros((27, 4), np.int32)
    base = np.zeros((27, 4), np.int32)
    for t in range(27):
        a, b, e = t // 9, t // 3 % 3, t % 3
        for c in range(4):
            y, x = c // 2 + b - 1, c % 2 + e - 1
            by, bx = y // 2 + 1, x // 2 + 1
            block[t, c] = 9 * a + 3 * by + bx
            base[t, c] = (3 * a + by) * 16 + (y % 2) * 2 + x % 2
    return block, base


def per_device(
    mesh_sizes, fine_input, cotangent, conv_weight, down_weight, depth_weight, up_weight, slot_x, neighbours
):
    B, S, H = mesh_sizes
    n = B * S * H
    reduce = n == 16 and H == 2
    nb = neighbours[0, 0]
    block, base = coarse_sources()
    hit = jnp.asarray(block)[:, None, :, None] == jnp.arange(27, dtype=jnp.int32)
    found = jnp.sum(jnp.where(hit, nb[None, :, None, :], 0), axis=-1)
    idx = jnp.where(found >= 0, jnp.asarray(base)[:, None, :] + 4 * found, -1).reshape(432, 1)
    vm = pl.BlockSpec(memory_space=pltpu.VMEM)
    sm = pl.BlockSpec(memory_space=pltpu.SMEM)
    dma = pltpu.SemaphoreType.DMA
    V = pltpu.VMEM
    wide_rows = 8 if reduce else 128
    outs = pl.pallas_call(
        functools.partial(level_kernel, mesh_sizes, reduce),
        out_shape=(
            jax.ShapeDtypeStruct((4, 256, 128), BF16),
            jax.ShapeDtypeStruct((27, wide_rows, 128), F32),
            jax.ShapeDtypeStruct((128, 256), F32),
            jax.ShapeDtypeStruct((27, 256), F32),
            jax.ShapeDtypeStruct((256, 128), F32),
        ),
        in_specs=[sm] + [vm] * 7,
        out_specs=(vm,) * 5,
        scratch_shapes=[
            V((5, 4, 8, 8, 128), F32), V((2, 5, 8, 8, 128), F32), V((2, 5, 4, 8, 128), F32),
            V((4, 5, 8, 128), F32),
            V((2, 2, 256, 128), BF16), V((2, 2, 128, 128), BF16), V((2, 4, 32, 128), BF16),
            V((2, 2, 256, 128), BF16), V((2, 2, 128, 128), BF16), V((2, 4, 32, 128), BF16),
            V((3, 6, 10, 8, 128), F32), V((6, 4, 64, 1152), BF16), V((4, 4, 64, 128), F32),
            V((4, 4, 64, 128), BF16), V((3, 1152, 128), BF16), V((2, 9, 16, 256), BF16),
            V((3, 10, 128, 128), F32),
            V((3, 8, 80, 128), BF16), V((3, 8, 80, 128), BF16),
            V((3, 8, 80, 128), BF16), V((3, 8, 80, 128), BF16),
            V((16, 48, 128), BF16), V((16, 48, 128), BF16), V((16, 48, 128), BF16),
            V((64, 128), F32),
            dma((2, 8)), dma((2, 8)), dma((2, 8)), dma((2, 8)),
            dma((3,)), dma((3,)), dma((3, 8)), dma((3, 8)),
            dma((16,)), dma((16,)), dma((16,)), dma((16,)),
        ],
        compiler_params=pltpu.CompilerParams(
            collective_id=0, has_side_effects=True, vmem_limit_bytes=48 * 1024 * 1024),
        name="level_pair",
    )(nb, fine_input[0, 0], cotangent[0, 0], conv_weight, down_weight, depth_weight, up_weight, idx)
    dx, cw, dn, dp, up = outs
    dx = dx.reshape(fine_input.shape)
    if reduce:
        cw = cw.reshape(27, 1024)
    else:
        axes = ("blk", "slab", "ch")
        dn, dp, up = lax.psum((dn, dp, up), axes)
        cw = lax.psum_scatter(cw.reshape(27, 128 * 128), axes, scatter_dimension=1, tiled=True)
    return dx, cw, dn, dp, up


def solution(mesh):
    sizes = (mesh.shape["blk"], mesh.shape["slab"], mesh.shape["ch"])
    fine = P(("groups", "slab", "ch"), "blk", None, None, None)
    in_specs = (
        fine, fine, P(), P(), P(), P(),
        P(("groups", "slab", "ch"), "blk", None),
        P(("groups", "slab", "ch"), "blk", None, None),
    )
    out_specs = (
        fine,
        P("groups", ("blk", "slab", "ch")),
        P("groups", None),
        P("groups", None),
        P("groups", None),
    )
    return jax.shard_map(
        functools.partial(per_device, sizes), mesh=mesh, in_specs=in_specs, out_specs=out_specs,
        check_vma=False)
```

time: 356 us -> 54 us (0.15)
  waiting for transfers between devices: 151 us -> 0 us
  blocking collectives: 61.9 us -> 0 us
  matrix products: 45.4 us -> 0 us
  Pallas kernels: 0 us -> 43.3 us
  starting transfers between devices: 36.8 us -> 0 us
  local copies, waits for them, and re-layouts: 29.6 us -> 6.28 us
  between operations: 16.2 us -> 0.75 us
  other arithmetic: 14.3 us -> 3.48 us
    reduce_scatter x1 -> x0, waiting for transfers between devices: 66.4 us -> none  [per_device(): lax.psum_scatter(weight_sum, ('blk', 'slab', 'ch'), scatter_dimension=1,...]
    psum x1 -> x0, waiting for transfers between devices: 62.8 us -> none  [per_device(): lax.psum((down_part, depth_part, up_part), ('blk', 'slab', 'ch'))]
    psum x1 -> x0, blocking collectives: 61.9 us -> none  [per_device(): lax.psum((down_part, depth_part, up_part), ('blk', 'slab', 'ch'))]
    dot_general x90 -> x0, matrix products: 45.4 us -> none  [the longest x27 27.8 us: per_device(): lax.dot_general(tap_slice(tiles, index, False), grad_flat, (((0,), (0,)),...]
    pallas_call x0 -> x1, Pallas kernels: none -> 43.3 us  [per_device(): pl.pallas_call(functools.partial(level_kernel, mesh_sizes, reduce), out_s...]
    ppermute x16 -> x0, starting transfers between devices: 36.5 us -> none  [the longest x8 26 us: with_halo(): before = lax.ppermute(last, axis, up)]
    ppermute x16 -> x0, waiting for transfers between devices: 21.6 us -> none  [the longest x8 17.9 us: with_halo(): after = lax.ppermute(leading, axis, down)]
    slice x64 -> x0, local copies, waits for them, and re-layouts: 10.1 us -> none  [the longest x58 8.29 us: tap_slice(): tiles[:, start_z:start_z + 4, start_y:start_y + 8, start_x:start_x + 8]]
  transfers between devices with their start and end apart: 18 -> 0, of which waited for: 10 -> 0; matrix products, arithmetic and copies ran while one was open for 9% -> 0% of each run, Pallas kernels for 0% -> 0%
where the time goes in v1:
time: 54 us; the launch traced here: 53.8 us
  Pallas kernels  43.3 us (80%)
  local copies, waits for them, and re-layouts  6.28 us (12%)
  other arithmetic  3.48 us (6%)
  between operations  0.75 us (1%)
    pallas_call x1, Pallas kernels, per_device(): pl.pallas_call(functools.partial(level_kernel, mesh_sizes, reduce), out_s...  43.3 us
    unnamed x22, local copies, waits for them, and re-layouts  6.15 us
    reduce_sum x1, other arithmetic, per_device(): found = jnp.sum(jnp.where(hit, nb[None, :, None, :], 0), axis=-1)  2.6 us

profile of v1, /device:TPU:0, one launch (start us, length us, event | category | flops | bytes accessed | tf_op | source)
XLA Modules:
  0.0 53.8 jit_solution(9690514352916083452)
XLA Ops:
  0.6 0.0 copy-start.7
  0.6 0.0 copy-start.1
  0.7 0.9 %iota_compare_fusion = pred[27,4,27]{2,1,0:T(4,128)(4,1)S(1)} fusion(s32[27,4]{1,0:T(8,128)} %constant.4.clone), kind=kLoop, calls=%fused_computation.2 | loop fusion | flops 2916 | bytes 3348 | tf_op jit(solution)/shard_map/eq | solution.py:369
  1.5 2.6 %select_reduce_fusion = s32[27,4,4]{2,1,0:T(4,128)S(1)} fusion(s32[4,27]{1,0:T(4,128)} %bitcast.10, pred[27,4,27]{2,1,0:T(4,128)(4,1)S(1)} %iota_compare_fusion), kind=kLoop, calls=%fused_computation | loop fusion | flops 22896 | bytes 5076 | tf_op jit(solution)/shard_map/reduce_sum | solution.py:370
  4.1 0.0 copy-done.7
  4.2 0.0 copy-start.3
  4.2 0.0 copy-start.4
  4.2 0.0 copy-start.5
  4.2 0.0 copy-start.6
  4.2 0.1 select_n.21.idx_in
  4.3 0.0 copy-done.1
  4.4 0.7 %copy-done.3 = bf16[128,256]{1,0:T(8,128)(2,1)S(1)} copy-done((bf16[128,256]{1,0:T(8,128)(2,1)S(1)}, bf16[128,256]{1,0:T(8,128)(2,1)}, u32[]{:S(2)}) %copy-start.3) | copy-done | bytes 65560
  5.0 0.0 copy-done.4
  5.0 0.0 copy-done.5
  5.0 0.0 copy-done.6
  5.0 0.0 copy-start
  5.0 1.2 %copy-done = bf16[27,128,128]{2,1,0:T(8,128)(2,1)S(1)} copy-done((bf16[27,128,128]{2,1,0:T(8,128)(2,1)S(1)}, bf16[27,128,128]{2,1,0:T(8,128)(2,1)}, u32[]{:S(2)}) %copy-start) | copy-done | bytes 884760
  6.2 0.9 %copy-done.2 = bf16[1,1,4,256,128]{4,3,2,1,0:T(8,128)(2,1)S(1)} copy-done((bf16[1,1,4,256,128]{4,3,2,1,0:T(8,128)(2,1)S(1)}, bf16[1,1,4,256,128]{4,3,2,1,0:T(8,128)(2,1)}, u32[]{:S(2)}) %copy-start.2) | copy-done | bytes 262168
  7.2 43.3 %level_pair.1 = (bf16[4,256,128]{2,1,0:T(8,128)(2,1)S(1)}, f32[27,8,128]{2,1,0:T(8,128)S(1)}, f32[128,256]{1,0:T(8,128)S(1)}, f32[27,256]{1,0:T(8,128)S(1)}, f32[256,128]{1,0:T(8,128)S(1)}) custom-call(s32[4,27]{1,0:T(4,128)S(1)} %bitcast.11, bf16[4,256,128]{2,1,0:T(8,128)(2,1)S(1)} %bitcast.8, bf16[4,256,128]{2,1,0:T(8,128)(2,1)S(1)} %bitcast.9, ...), custom_call_target="tpu_custom_call" | custom-call | tf_op jit(solution)/shard_map/level_pair/pallas_call | solution.py:377
  50.5 0.7 %copy.16 = f32[4,8,8,128]{3,1,2,0:T(8,128)} copy(f32[4,8,8,128]{3,2,1,0:T(8,128)S(1)} %bitcast.12) | data formatting | bytes 262144
  51.1 0.7 %copy.21 = bf16[1,1,4,256,128]{4,3,2,1,0:T(8,128)(2,1)} copy(bf16[1,1,4,256,128]{4,3,2,1,0:T(8,128)(2,1)S(1)} %bitcast.7) | data formatting | bytes 524288
  51.8 0.7 %copy.22 = f32[128,256]{1,0:T(8,128)} copy(f32[128,256]{1,0:T(8,128)S(1)} %get-tuple-element.22) | data formatting | bytes 262144
  52.5 0.6 %copy.23 = f32[27,256]{1,0:T(8,128)} copy(f32[27,256]{1,0:T(8,128)S(1)} %get-tuple-element.23) | data formatting | bytes 55296
  53.1 0.7 %copy.24 = f32[256,128]{1,0:T(8,128)} copy(f32[256,128]{1,0:T(8,128)S(1)} %get-tuple-element.24) | data formatting | bytes 262144
  (3 shorter events, 0.0 us)
Async XLA Ops:
  0.6 3.5 %copy-start.7 = (s32[27,4]{1,0:T(8,128)S(1)}, s32[27,4]{1,0:T(8,128)}, u32[]{:S(2)}) copy-start(s32[27,4]{1,0:T(8,128)} %constant.12.clone) | copy-start | bytes 1300
  0.6 3.7 %copy-start.1 = (bf16[1,1,4,256,128]{4,3,2,1,0:T(8,128)(2,1)S(1)}, bf16[1,1,4,256,128]{4,3,2,1,0:T(8,128)(2,1)}, u32[]{:S(2)}) copy-start(bf16[1,1,4,256,128]{4,3,2,1,0:T(8,128)(2,1)} %param.10) | copy-start | bytes 786436
  4.2 0.8 %copy-start.3 = (bf16[128,256]{1,0:T(8,128)(2,1)S(1)}, bf16[128,256]{1,0:T(8,128)(2,1)}, u32[]{:S(2)}) copy-start(bf16[128,256]{1,0:T(8,128)(2,1)} %down_w.1) | copy-start | bytes 196612
  4.2 0.9 %copy-start.4 = (bf16[256,128]{1,0:T(8,128)(2,1)S(1)}, bf16[256,128]{1,0:T(8,128)(2,1)}, u32[]{:S(2)}) copy-start(bf16[256,128]{1,0:T(8,128)(2,1)} %up_w.1) | copy-start | bytes 196612
  4.2 0.9 %copy-start.5 = (bf16[27,256]{1,0:T(8,128)(2,1)S(1)}, bf16[27,256]{1,0:T(8,128)(2,1)}, u32[]{:S(2)}) copy-start(bf16[27,256]{1,0:T(8,128)(2,1)} %depth_w.1) | copy-start | bytes 41476
  4.2 0.8 %copy-start.6 = (s32[1,1,4,27]{3,2,1,0:T(4,128)S(1)}, s32[1,1,4,27]{3,2,1,0:T(4,128)}, u32[]{:S(2)}) copy-start(s32[1,1,4,27]{3,2,1,0:T(4,128)} %param.16) | copy-start | bytes 1300
  5.0 1.2 %copy-start = (bf16[27,128,128]{2,1,0:T(8,128)(2,1)S(1)}, bf16[27,128,128]{2,1,0:T(8,128)(2,1)}, u32[]{:S(2)}) copy-start(bf16[27,128,128]{2,1,0:T(8,128)(2,1)} %conv_w.1) | copy-start | bytes 2654212
  6.2 0.9 %copy-start.2 = (bf16[1,1,4,256,128]{4,3,2,1,0:T(8,128)(2,1)S(1)}, bf16[1,1,4,256,128]{4,3,2,1,0:T(8,128)(2,1)}, u32[]{:S(2)}) copy-start(bf16[1,1,4,256,128]{4,3,2,1,0:T(8,128)(2,1)} %param.11) | copy-start | bytes 786436

commit v2 on v1

--- a/solution.py
+++ b/solution.py
@@ -2,7 +2,6 @@
 
 import jax
 import jax.numpy as jnp
-import numpy as np
 from jax import lax
 from jax.experimental import pallas as pl
 from jax.experimental.pallas import tpu as pltpu
@@ -20,11 +19,12 @@
 
 
 def level_kernel(
-    sizes, reduce, nb, x_in, cot_in, conv_w, down_w, depth_w, up_w, idx_in,
+    sizes, reduce, nb, nbv, depth_w, x_hbm, cot_hbm, conv_hbm, down_hbm, up_hbm,
     dx_out, cw_out, dn_out, dp_out, up_out,
     C0, NZ, NY, NC, hz, hy, hc, sz, sy, sc, FR, T, FS, DF, WB, GA, WF,
-    st1, rv1, st2, rv2, sms, smr, ag, DG,
-    hs, hr, cs, cr, p1s, p1r, p2s, p2r, ss, sr, gs, gr,
+    st10, st11, st12, rv10, rv11, rv12, st20, st21, st22, rv20, rv21, rv22,
+    st30, st31, st32, rv30, rv31, rv32, ag, DG, SMALL, x_in, cot_in, conv_w, down_w, up_w,
+    hs, hr, cs, cr, p1s, p1r, p2s, p2r, p3s, p3r, gs, gr, ls,
 ):
     B, S, H = sizes
     K = 4
@@ -44,7 +44,12 @@
     def beside(da, db):
         return target((blk + db) * rows + row + da)
 
-    for ref in (hz, hy, hc, GA, sms):
+    pulls = [pltpu.make_async_copy(src, dst, ls.at[i]) for i, (src, dst) in enumerate((
+        (x_hbm, x_in), (cot_hbm, cot_in), (conv_hbm, conv_w), (up_hbm, up_w), (down_hbm, down_w)))]
+    for pull in pulls:
+        pull.start()
+
+    for ref in (hz, hy, hc, GA):
         ref[...] = jnp.zeros(ref.shape, ref.dtype)
     C0[K] = jnp.zeros(C0.shape[1:], F32)
     NZ[:, K] = jnp.zeros((2,) + NZ.shape[2:], F32)
@@ -154,11 +159,14 @@
 
         lax.fori_loop(0, K, slot, 0)
 
+    pulls[0].wait()
     C0[0:K] = x_in[...].astype(F32).reshape(K, 4, 8, 8, 128)
     stage(0)
     entered()
     send_halo(0)
 
+    for pull in pulls[1:]:
+        pull.wait()
     for a in range(3):
         for t in range(9):
             WB[a, 128 * t:128 * t + 128, :] = conv_w[26 - 9 * a - t].astype(F32).T.astype(BF16)
@@ -174,8 +182,33 @@
          for k in range(K)], axis=0).reshape(64, 128)
     dz = jnp.dot(pool, cot_rows, precision=HIGH, preferred_element_type=F32).astype(BF16)
     grad_q = lax.dot_general(dz, up_w[...], (((1,), (1,)), ((), ())), preferred_element_type=F32)
-    pick = (idx_in[...] == lax.broadcasted_iota(jnp.int32, (432, 144), 1)).astype(F32).astype(BF16)
-    depth = depth_w[...].astype(F32)
+    depth = jnp.concatenate([depth_w[...].astype(F32), jnp.zeros((5, 256), F32)], axis=0)
+    turn_r = lax.broadcasted_iota(jnp.int32, (32, 32), 0)
+    turn_c = lax.broadcasted_iota(jnp.int32, (32, 32), 1)
+    turned = jnp.dot((turn_r + turn_c == 26).astype(F32), depth, precision=HIGH,
+                     preferred_element_type=F32)
+
+    def source(c, shape):
+        t = lax.broadcasted_iota(jnp.int32, shape, 0)
+        ys, xs = t // 3 % 3 + c // 2 + 1, t % 3 + c % 2 + 1
+        block = 9 * (t // 9) + 3 * (ys // 2) + xs // 2
+        base = (3 * (t // 9) + ys // 2) * 16 + ys % 2 * 2 + xs % 2
+        return t, block, base
+
+    found = []
+    for c in range(4):
+        t, block, _ = source(c, (32, 27))
+        hit = ((block == lax.broadcasted_iota(jnp.int32, (32, 27), 1)) & (t < 27)).astype(F32)
+        found.append(lax.dot_general(hit, nbv[...].astype(F32), (((1,), (1,)), ((), ())),
+                                     precision=HIGH, preferred_element_type=F32))
+    picks = []
+    for k in range(K):
+        for c in range(4):
+            t, _, base = source(c, (32, 144))
+            col = (lax.broadcasted_iota(jnp.int32, (32, 144), 1) - base).astype(F32)
+            slot_of = found[c][:, k:k + 1]
+            picks.append(((col == 4.0 * slot_of) & (slot_of >= 0.0) & (t < 27)).astype(F32))
+    pick = jnp.concatenate(picks, axis=0).astype(BF16)
     WF[:, 9] = jnp.zeros((3, 128, 128), F32)
 
     wait_halo(0)
@@ -196,29 +229,22 @@
     GA[0, 4] = g
     send_coarse(0)
     wait_coarse(0)
-    near = jnp.dot(pick, GA[0].reshape(144, 256), preferred_element_type=F32)
-    v = jnp.zeros((16, 256), F32)
-    for t in range(27):
-        v = v + near[16 * t:16 * t + 16] * depth[t:t + 1]
-    v = v + g.astype(F32)
+    near = jnp.dot(pick, GA[0].reshape(144, 256), preferred_element_type=F32).reshape(16, 32, 256)
+    v = g.astype(F32) + jnp.sum(near * depth[None], axis=1)
     dv = (grad_q * silu_slope(v)).astype(BF16)
     GA[1, 4] = dv
     send_coarse(1)
     dvf = dv.astype(F32)
     q = (v * jax.nn.sigmoid(v)).astype(BF16)
     up_part = lax.dot_general(q, dz, (((0,), (0,)), ((), ())), preferred_element_type=F32)
-    DG[...] = jnp.zeros(DG.shape, F32)
-    for t in range(27):
-        line = jnp.sum(near[16 * t:16 * t + 16] * dvf, axis=0, keepdims=True)
-        DG[t:t + 1] = line[:, :128]
-        DG[32 + t:33 + t] = line[:, 128:]
+    lines = near[0] * dvf[0:1]
+    for c in range(1, 16):
+        lines = lines + near[c] * dvf[c:c + 1]
+    DG[0:32] = lines[:, :128]
+    DG[32:64] = lines[:, 128:]
     wait_coarse(1)
-    near = jnp.dot(pick, GA[1].reshape(144, 256), preferred_element_type=F32)
-    dg = jnp.zeros((16, 256), F32)
-    for t in range(27):
-        u = 26 - t
-        dg = dg + near[16 * u:16 * u + 16] * depth[t:t + 1]
-    dg = (dg + dvf).astype(BF16)
+    near = jnp.dot(pick, GA[1].reshape(144, 256), preferred_element_type=F32).reshape(16, 32, 256)
+    dg = (jnp.sum(near * turned[None], axis=1) + dvf).astype(BF16)
     dp = lax.dot_general(dg, down_w[...], (((1,), (1,)), ((), ())), preferred_element_type=F32)
     wide = jnp.dot(unpool, dp * (1.0 / 64.0), precision=HIGH, preferred_element_type=F32)
     wide = wide.reshape(K, 2, 8, 128)
@@ -232,92 +258,121 @@
     send_halo(1)
     down_part = lax.dot_general(p, dg, (((0,), (0,)), ((), ())), preferred_element_type=F32)
 
+    st1, rv1 = (st10, st11, st12), (rv10, rv11, rv12)
+    st2, rv2 = (st20, st21, st22), (rv20, rv21, rv22)
+    st3, rv3 = (st30, st31, st32), (rv30, rv31, rv32)
+    Q = B * S
+    mine = blk * S + slab
+
+    def each(count, fn):
+        def body(r, carry):
+            fn(r)
+            return carry
+        lax.fori_loop(1, count, body, 0)
+
+    def at_chip(q):
+        return {"blk": lax.div(q, S), "slab": lax.rem(q, S), "ch": ch}
+
+    def across(a):
+        return copy(st1[a], rv1[a], p1s.at[a], p1r.at[a],
+                    {"blk": blk, "slab": slab, "ch": 1 - ch})
+
+    def along_slab(a):
+        return copy(st2[a].at[1 - slab], rv2[a], p2s.at[a], p2r.at[a],
+                    {"blk": blk, "slab": 1 - slab, "ch": ch})
+
+    def along_blk(a, r):
+        to = lax.rem(blk + r, B)
+        return copy(st3[a].at[to], rv3[a].at[blk], p3s.at[a, r], p3r.at[a, r],
+                    {"blk": to, "slab": slab, "ch": ch})
+
+    def from_blk(a, r):
+        src = lax.rem(blk - r + B, B)
+        return copy(st3[a].at[src], rv3[a].at[src], p3s.at[a, r], p3r.at[a, r],
+                    {"blk": src, "slab": slab, "ch": ch})
+
+    def gather_out(r):
+        to = lax.rem(mine + r, Q)
+        return copy(ag.at[ch, mine], ag.at[ch, mine], gs.at[r], gr.at[r], at_chip(to))
+
+    def gather_in(r):
+        src = lax.rem(mine - r + Q, Q)
+        return copy(ag.at[ch, src], ag.at[ch, src], gs.at[r], gr.at[r], at_chip(src))
+
+    def gather_pair(side):
+        return copy(ag.at[side], ag.at[side], gs.at[0], gr.at[0],
+                    {"blk": blk, "slab": slab, "ch": 1 - ch})
+
+    def step_core(a):
+        for sl in range(S):
+            for bk in range(B):
+                at = pl.multiple_of(8 * ((bk * S + sl) * 2 + 1 - ch), 8)
+                st1[a][sl, bk, 0:80] = WF[a, :, pl.ds(at, 8)].reshape(80, 128).astype(BF16)
+        across(a).start()
+
+    def step_slab(a):
+        across(a).wait()
+        for sl in range(S):
+            for bk in range(B):
+                at = pl.multiple_of(8 * ((bk * S + sl) * 2 + ch), 8)
+                st2[a][sl, bk, 0:80] = (WF[a, :, pl.ds(at, 8)].reshape(80, 128)
+                                        + rv1[a][sl, bk, 0:80].astype(F32)).astype(BF16)
+                if a == 0:
+                    st2[a][sl, bk, 80:128] = (SMALL[2 * (bk * S + sl) + ch]
+                                              + rv1[a][sl, bk, 80:128].astype(F32)).astype(BF16)
+        along_slab(a).start()
+
+    def step_blk(a):
+        along_slab(a).wait()
+        st3[a][...] = (st2[a][slab].astype(F32) + rv2[a][...].astype(F32)).astype(BF16)
+        each(B, lambda r: along_blk(a, r).start())
+
+    def step_sum(a):
+        each(B, lambda r: from_blk(a, r).wait())
+        rv3[a][blk] = st3[a][blk]
+        total = rv3[a][0].astype(F32)
+        for bk in range(1, B):
+            total = total + rv3[a][bk].astype(F32)
+        cw_out[9 * a:9 * a + 9] = total[0:80].reshape(10, 8, 128)[0:9]
+        return total
+
     if reduce:
-        sms[:, 0:16] = up_part.reshape(16, 16, 128).astype(BF16)
-        sms[0:8, 16:32] = down_part[:, :128].reshape(8, 16, 128).astype(BF16)
-        sms[8:16, 16:32] = down_part[:, 128:].reshape(8, 16, 128).astype(BF16)
-        sms[0:4, 32:48] = DG[...].reshape(4, 16, 128).astype(BF16)
-
-        def small(r):
-            to = lax.rem(me + r, n)
-            return copy(sms.at[to], smr.at[me], ss.at[r], sr.at[r], target(to))
-
-        def small_in(r):
-            src = lax.rem(me - r + n, n)
-            return copy(sms.at[src], smr.at[src], ss.at[r], sr.at[r], target(src))
-
-        def final(r):
-            to = lax.rem(me + r, n)
-            return copy(ag.at[me], ag.at[me], gs.at[r], gr.at[r], target(to))
-
-        def final_in(r):
-            src = lax.rem(me - r + n, n)
-            return copy(ag.at[src], ag.at[src], gs.at[r], gr.at[r], target(src))
-
-        def each(count, fn):
-            def body(r, carry):
-                fn(r)
-                return carry
-            lax.fori_loop(1, count, body, 0)
-
-        each(n, lambda r: small(r).start())
+        SMALL[:, 0:16] = up_part.reshape(16, 16, 128)
+        SMALL[0:8, 16:32] = down_part[:, :128].reshape(8, 16, 128)
+        SMALL[8:16, 16:32] = down_part[:, 128:].reshape(8, 16, 128)
+        SMALL[0:4, 32:48] = DG[...].reshape(4, 16, 128)
+        SMALL[4:16, 32:48] = jnp.zeros((12, 16, 128), F32)
+        for sl in range(S):
+            for bk in range(B):
+                st10[sl, bk, 80:128] = SMALL[2 * (bk * S + sl) + 1 - ch].astype(BF16)
     else:
         up_out[...] = up_part
         dn_out[...] = down_part
         dp_out[:, :128] = DG[0:27]
         dp_out[:, 128:] = DG[32:59]
 
-    Q = B * S
-    mine = blk * S + slab
-    other = 1 - ch
-
-    def pair(a):
-        return copy(st1.at[a], rv1.at[a], p1s.at[a], p1r.at[a],
-                    {"blk": blk, "slab": slab, "ch": other})
-
-    def spread_to(a, r):
-        to = lax.rem(mine + r, Q)
-        return copy(st2.at[a, to], rv2.at[a, mine], p2s.at[a, r], p2r.at[a, r],
-                    {"blk": lax.div(to, S), "slab": lax.rem(to, S), "ch": ch})
-
-    def spread_in(a, r):
-        src = lax.rem(mine - r + Q, Q)
-        return copy(st2.at[a, src], rv2.at[a, src], p2s.at[a, r], p2r.at[a, r],
-                    {"blk": lax.div(src, S), "slab": lax.rem(src, S), "ch": ch})
-
-    def forward_pair(a):
-        pair(a).wait()
-        for qi in range(Q):
-            at = pl.multiple_of(8 * (2 * qi + ch), 8)
-            st2[a, qi] = (WF[a, :, pl.ds(at, 8)].reshape(80, 128)
-                          + rv1[a, qi].astype(F32)).astype(BF16)
-        each(Q, lambda r: spread_to(a, r).start())
-
     for a in range(3):
         wg = lax.dot_general(T[a:a + 4].reshape(1024, 1152), DF[...].reshape(1024, 128),
                              (((0,), (0,)), ((), ())), preferred_element_type=F32)
-        WF[a, 0:9] = wg.reshape(9, 128, 128)
         if reduce:
-            for qi in range(Q):
-                at = pl.multiple_of(8 * (2 * qi + other), 8)
-                st1[a, qi] = WF[a, :, pl.ds(at, 8)].reshape(80, 128).astype(BF16)
-            pair(a).start()
+            WF[a, 0:9] = wg.reshape(9, 128, 128)
+            step_core(a)
             if a > 0:
-                forward_pair(a - 1)
+                step_slab(a - 1)
+            if a > 1:
+                step_blk(a - 2)
         else:
             cw_out[9 * a:9 * a + 9] = wg.reshape(9, 128, 128)
     if reduce:
-        each(n, lambda r: small_in(r).wait())
-        smr[me] = sms[me]
-        total = smr[0].astype(F32)
-        for d in range(1, 16):
-            total = total + smr[d].astype(F32)
-        ag[me] = total.astype(BF16)
-        each(n, lambda r: final(r).start())
-        forward_pair(2)
+        step_slab(2)
+        step_blk(1)
 
     wait_halo(1)
     build()
+    if reduce:
+        step_blk(2)
+        ag[ch, mine] = step_sum(0)[80:128].astype(BF16)
+        each(Q, lambda r: gather_out(r).start())
     for a in range(3):
         term = jnp.dot(T[a:a + 4].reshape(1024, 1152), WB[a],
                        preferred_element_type=F32).reshape(4, K, 64, 128)
@@ -329,33 +384,34 @@
         dx_out[k] = FS[:, k].reshape(256, 128).astype(BF16)
 
     if reduce:
-        each(n, lambda r: final_in(r).wait())
-        up_out[...] = ag[:, 0:16].astype(F32).reshape(256, 128)
-        dn_out[:, :128] = ag[0:8, 16:32].astype(F32).reshape(128, 128)
-        dn_out[:, 128:] = ag[8:16, 16:32].astype(F32).reshape(128, 128)
-        DG[...] = ag[0:4, 32:48].astype(F32).reshape(64, 128)
+        step_sum(1)
+        each(Q, lambda r: gather_in(r).wait())
+        gather_pair(ch).start()
+        step_sum(2)
+        gather_pair(1 - ch).wait()
+        for c in range(2):
+            for qi in range(8):
+                d = 2 * qi + c
+                up_out[16 * d:16 * d + 16] = ag[c, qi, 0:16].astype(F32)
+                at, side = 16 * (d % 8), 128 * (d // 8)
+                dn_out[at:at + 16, side:side + 128] = ag[c, qi, 16:32].astype(F32)
+                if d < 4:
+                    DG[16 * d:16 * d + 16] = ag[c, qi, 32:48].astype(F32)
         dp_out[:, :128] = DG[0:27]
         dp_out[:, 128:] = DG[32:59]
-        for a in range(3):
-            each(Q, lambda r: spread_in(a, r).wait())
-            rv2[a, mine] = st2[a, mine]
-            total = rv2[a, 0].astype(F32)
-            for qi in range(1, 8):
-                total = total + rv2[a, qi].astype(F32)
-            cw_out[9 * a:9 * a + 9] = total.reshape(10, 8, 128)[0:9]
-
-
-def coarse_sources():
-    block = np.zeros((27, 4), np.int32)
-    base = np.zeros((27, 4), np.int32)
-    for t in range(27):
-        a, b, e = t // 9, t // 3 % 3, t % 3
-        for c in range(4):
-            y, x = c // 2 + b - 1, c % 2 + e - 1
-            by, bx = y // 2 + 1, x // 2 + 1
-            block[t, c] = 9 * a + 3 * by + bx
-            base[t, c] = (3 * a + by) * 16 + (y % 2) * 2 + x % 2
-    return block, base
+
+
+def write_kernel(dx, cw, dn, dp, up, dx_o, cw_o, dn_o, dp_o, up_o, flat, sem):
+    moves = [pltpu.make_async_copy(src, dst, sem.at[i])
+             for i, (src, dst) in enumerate(((dx, dx_o), (dn, dn_o), (dp, dp_o), (up, up_o)))]
+    for move in moves:
+        move.start()
+    for i in range(8):
+        flat[:, 128 * i:128 * i + 128] = cw[:, i, :]
+    moves.append(pltpu.make_async_copy(flat, cw_o, sem.at[4]))
+    moves[4].start()
+    for move in moves:
+        move.wait()
 
 
 def per_device(
@@ -363,17 +419,14 @@
 ):
     B, S, H = mesh_sizes
     n = B * S * H
-    reduce = n == 16 and H == 2
+    reduce = (B, S, H) == (4, 2, 2)
     nb = neighbours[0, 0]
-    block, base = coarse_sources()
-    hit = jnp.asarray(block)[:, None, :, None] == jnp.arange(27, dtype=jnp.int32)
-    found = jnp.sum(jnp.where(hit, nb[None, :, None, :], 0), axis=-1)
-    idx = jnp.where(found >= 0, jnp.asarray(base)[:, None, :] + 4 * found, -1).reshape(432, 1)
     vm = pl.BlockSpec(memory_space=pltpu.VMEM)
     sm = pl.BlockSpec(memory_space=pltpu.SMEM)
     dma = pltpu.SemaphoreType.DMA
     V = pltpu.VMEM
     wide_rows = 8 if reduce else 128
+    part_rows = (128, 80, 80)
     outs = pl.pallas_call(
         functools.partial(level_kernel, mesh_sizes, reduce),
         out_shape=(
@@ -383,7 +436,7 @@
             jax.ShapeDtypeStruct((27, 256), F32),
             jax.ShapeDtypeStruct((256, 128), F32),
         ),
-        in_specs=[sm] + [vm] * 7,
+        in_specs=[sm, vm, vm] + [pl.BlockSpec(memory_space=pl.ANY)] * 5,
         out_specs=(vm,) * 5,
         scratch_shapes=[
             V((5, 4, 8, 8, 128), F32), V((2, 5, 8, 8, 128), F32), V((2, 5, 4, 8, 128), F32),
@@ -393,27 +446,40 @@
             V((3, 6, 10, 8, 128), F32), V((6, 4, 64, 1152), BF16), V((4, 4, 64, 128), F32),
             V((4, 4, 64, 128), BF16), V((3, 1152, 128), BF16), V((2, 9, 16, 256), BF16),
             V((3, 10, 128, 128), F32),
-            V((3, 8, 80, 128), BF16), V((3, 8, 80, 128), BF16),
-            V((3, 8, 80, 128), BF16), V((3, 8, 80, 128), BF16),
-            V((16, 48, 128), BF16), V((16, 48, 128), BF16), V((16, 48, 128), BF16),
-            V((64, 128), F32),
+            *[V((2, B, rows, 128), BF16) for rows in part_rows],
+            *[V((2, B, rows, 128), BF16) for rows in part_rows],
+            *[V((2, B, rows, 128), BF16) for rows in part_rows],
+            *[V((B, rows, 128), BF16) for rows in part_rows],
+            *[V((B, rows, 128), BF16) for rows in part_rows],
+            *[V((B, rows, 128), BF16) for rows in part_rows],
+            V((2, 8, 48, 128), BF16),
+            V((64, 128), F32), V((16, 48, 128), F32),
+            V((4, 256, 128), BF16), V((4, 256, 128), BF16), V((27, 128, 128), BF16),
+            V((128, 256), BF16), V((256, 128), BF16),
             dma((2, 8)), dma((2, 8)), dma((2, 8)), dma((2, 8)),
-            dma((3,)), dma((3,)), dma((3, 8)), dma((3, 8)),
-            dma((16,)), dma((16,)), dma((16,)), dma((16,)),
+            dma((3,)), dma((3,)), dma((3,)), dma((3,)), dma((3, 4)), dma((3, 4)),
+            dma((8,)), dma((8,)), dma((5,)),
         ],
         compiler_params=pltpu.CompilerParams(
             collective_id=0, has_side_effects=True, vmem_limit_bytes=48 * 1024 * 1024),
         name="level_pair",
-    )(nb, fine_input[0, 0], cotangent[0, 0], conv_weight, down_weight, depth_weight, up_weight, idx)
+    )(nb, nb, depth_weight, fine_input[0, 0], cotangent[0, 0], conv_weight, down_weight, up_weight)
     dx, cw, dn, dp, up = outs
-    dx = dx.reshape(fine_input.shape)
     if reduce:
-        cw = cw.reshape(27, 1024)
+        hbm = pl.BlockSpec(memory_space=pl.ANY)
+        dx, cw, dn, dp, up = pl.pallas_call(
+            write_kernel,
+            out_shape=(dx, jax.ShapeDtypeStruct((27, 1024), F32), dn, dp, up),
+            in_specs=[vm] * 5,
+            out_specs=(hbm,) * 5,
+            scratch_shapes=[V((27, 1024), F32), dma((5,))],
+            name="write_out",
+        )(dx, cw, dn, dp, up)
     else:
         axes = ("blk", "slab", "ch")
         dn, dp, up = lax.psum((dn, dp, up), axes)
         cw = lax.psum_scatter(cw.reshape(27, 128 * 128), axes, scatter_dimension=1, tiled=True)
-    return dx, cw, dn, dp, up
+    return dx.reshape(fine_input.shape), cw, dn, dp, up
 
 
 def solution(mesh):

time: 54 us -> 53.2 us (0.985)
  other arithmetic: 3.48 us -> 0 us
  local copies, waits for them, and re-layouts: 6.28 us -> 9.37 us
    unnamed x22 -> x24, local copies, waits for them, and re-layouts: 6.15 us -> 9.37 us
    reduce_sum x1 -> x0, other arithmetic: 2.6 us -> none  [per_device(): found = jnp.sum(jnp.where(hit, nb[None, :, None, :], 0), axis=-1)]
    pallas_call x1, Pallas kernels: 43.3 us -> 40.8 us  [per_device(): pl.pallas_call(functools.partial(level_kernel, mesh_sizes, reduce), out_s...]
    pallas_call x0 -> x1, Pallas kernels: none -> 2 us  [per_device(): pl.pallas_call(write_kernel, out_shape=(dx, jax.ShapeDtypeStruct((27, 102...]
    eq x1 -> x0, other arithmetic: 0.86 us -> none  [per_device(): jnp.asarray(block)[:, None, :, None] == jnp.arange(27, dtype=jnp.int32)]
where the time goes in v2:
time: 53.2 us; the launch traced here: 52.8 us
  Pallas kernels  42.8 us (80%)
  local copies, waits for them, and re-layouts  9.37 us (18%)
  between operations  0.67 us (1%)
    pallas_call x1, Pallas kernels, per_device(): pl.pallas_call(functools.partial(level_kernel, mesh_sizes, reduce), out_s...  40.8 us
    unnamed x24, local copies, waits for them, and re-layouts  9.37 us
    pallas_call x1, Pallas kernels, per_device(): pl.pallas_call(write_kernel, out_shape=(dx, jax.ShapeDtypeStruct((27, 102...  2 us

profile of v2, /device:TPU:0, one launch (start us, length us, event | category | flops | bytes accessed | tf_op | source)
XLA Modules:
  0.0 52.8 jit_solution(2075933545467666523)
XLA Ops:
  0.6 0.0 copy-start.11
  0.6 0.7 %copy-done.11 = s32[1,1,4,27]{3,2,1,0:T(4,128)S(1)} copy-done((s32[1,1,4,27]{3,2,1,0:T(4,128)S(1)}, s32[1,1,4,27]{3,2,1,0:T(4,128)}, u32[]{:S(2)}) %copy-start.11) | copy-done | bytes 456
  1.3 0.0 copy-start
  1.3 1.2 %copy-done = bf16[27,128,128]{2,1,0:T(8,128)(2,1)S(1)} copy-done((bf16[27,128,128]{2,1,0:T(8,128)(2,1)S(1)}, bf16[27,128,128]{2,1,0:T(8,128)(2,1)}, u32[]{:S(2)}) %copy-start) | copy-done | bytes 884760
  2.5 0.0 copy-start.1
  2.5 0.9 %copy-done.1 = bf16[1,1,4,256,128]{4,3,2,1,0:T(8,128)(2,1)S(1)} copy-done((bf16[1,1,4,256,128]{4,3,2,1,0:T(8,128)(2,1)S(1)}, bf16[1,1,4,256,128]{4,3,2,1,0:T(8,128)(2,1)}, u32[]{:S(2)}) %copy-start.1) | copy-done | bytes 262168
  3.4 0.9 %copy-done.2 = bf16[1,1,4,256,128]{4,3,2,1,0:T(8,128)(2,1)S(1)} copy-done((bf16[1,1,4,256,128]{4,3,2,1,0:T(8,128)(2,1)S(1)}, bf16[1,1,4,256,128]{4,3,2,1,0:T(8,128)(2,1)}, u32[]{:S(2)}) %copy-start.2) | copy-done | bytes 262168
  4.4 0.0 copy-start.7
  4.4 0.8 %copy-done.7 = bf16[128,256]{1,0:T(8,128)(2,1)S(1)} copy-done((bf16[128,256]{1,0:T(8,128)(2,1)S(1)}, bf16[128,256]{1,0:T(8,128)(2,1)}, u32[]{:S(2)}) %copy-start.7) | copy-done | bytes 65560
  5.2 0.0 copy-start.8
  5.2 0.8 %copy-done.8 = bf16[256,128]{1,0:T(8,128)(2,1)S(1)} copy-done((bf16[256,128]{1,0:T(8,128)(2,1)S(1)}, bf16[256,128]{1,0:T(8,128)(2,1)}, u32[]{:S(2)}) %copy-start.8) | copy-done | bytes 65560
  6.1 0.0 copy-start.10
  6.1 0.7 %copy-done.10 = bf16[27,256]{1,0:T(8,128)(2,1)S(1)} copy-done((bf16[27,256]{1,0:T(8,128)(2,1)S(1)}, bf16[27,256]{1,0:T(8,128)(2,1)}, u32[]{:S(2)}) %copy-start.10) | copy-done | bytes 13848
  6.8 40.8 %level_pair.1 = (bf16[4,256,128]{2,1,0:T(8,128)(2,1)S(1)}, f32[27,8,128]{2,1,0:T(8,128)S(1)}, f32[128,256]{1,0:T(8,128)S(1)}, f32[27,256]{1,0:T(8,128)S(1)}, f32[256,128]{1,0:T(8,128)S(1)}) custom-call(s32[4,27]{1,0:T(4,128)S(1)} %bitcast.6, s32[4,27]{1,0:T(4,128)S(1)} %bitcast.7, bf16[27,256]{1,0:T(8,128)(2,1)S(1)} %copy-done.10, ...), custom_call_target="tpu_custom_call" | custom-call | tf_op jit(solution)/shard_map/level_pair/pallas_call | solution.py:430
  47.5 0.0 copy-start.3
  47.6 0.7 %copy-done.3 = bf16[4,256,128]{2,1,0:T(8,128)(2,1)} copy-done((bf16[4,256,128]{2,1,0:T(8,128)(2,1)}, bf16[4,256,128]{2,1,0:T(8,128)(2,1)S(1)}, u32[]{:S(2)}) %copy-start.3) | copy-done | bytes 262168
  48.2 0.0 copy-start.4
  48.2 0.6 %copy-done.4 = f32[128,256]{1,0:T(8,128)} copy-done((f32[128,256]{1,0:T(8,128)}, f32[128,256]{1,0:T(8,128)S(1)}, u32[]{:S(2)}) %copy-start.4) | copy-done | bytes 131096
  48.9 0.0 copy-start.5
  48.9 0.6 %copy-done.5 = f32[256,128]{1,0:T(8,128)} copy-done((f32[256,128]{1,0:T(8,128)}, f32[256,128]{1,0:T(8,128)S(1)}, u32[]{:S(2)}) %copy-start.5) | copy-done | bytes 131096
  49.5 0.0 copy-start.6
  49.5 0.6 %copy-done.6 = f32[27,8,128]{2,1,0:T(8,128)} copy-done((f32[27,8,128]{2,1,0:T(8,128)}, f32[27,8,128]{2,1,0:T(8,128)S(1)}, u32[]{:S(2)}) %copy-start.6) | copy-done | bytes 110616
  50.2 0.6 %copy-done.9 = f32[27,256]{1,0:T(8,128)} copy-done((f32[27,256]{1,0:T(8,128)}, f32[27,256]{1,0:T(8,128)S(1)}, u32[]{:S(2)}) %copy-start.9) | copy-done | bytes 27672
  50.8 2.0 %write_out.1 = (bf16[4,256,128]{2,1,0:T(8,128)(2,1)}, f32[27,1024]{1,0:T(8,128)}, f32[128,256]{1,0:T(8,128)}, f32[27,256]{1,0:T(8,128)}, f32[256,128]{1,0:T(8,128)}) custom-call(bf16[4,256,128]{2,1,0:T(8,128)(2,1)} %copy-done.3, f32[27,8,128]{2,1,0:T(8,128)} %copy-done.6, f32[128,256]{1,0:T(8,128)} %copy-done.4, f32[27,256]{1,0:T(8,128)} %copy-done.9, ...), custom_call_target="tpu_custom_call" | custom-call | tf_op jit(solution)/shard_map/write_out/pallas_call | solution.py:470
  (2 shorter events, 0.0 us)
Async XLA Ops:
  0.6 0.7 %copy-start.11 = (s32[1,1,4,27]{3,2,1,0:T(4,128)S(1)}, s32[1,1,4,27]{3,2,1,0:T(4,128)}, u32[]{:S(2)}) copy-start(s32[1,1,4,27]{3,2,1,0:T(4,128)} %param.14) | copy-start | bytes 1300
  1.3 1.2 %copy-start = (bf16[27,128,128]{2,1,0:T(8,128)(2,1)S(1)}, bf16[27,128,128]{2,1,0:T(8,128)(2,1)}, u32[]{:S(2)}) copy-start(bf16[27,128,128]{2,1,0:T(8,128)(2,1)} %conv_hbm.1) | copy-start | bytes 2654212
  2.5 0.9 %copy-start.1 = (bf16[1,1,4,256,128]{4,3,2,1,0:T(8,128)(2,1)S(1)}, bf16[1,1,4,256,128]{4,3,2,1,0:T(8,128)(2,1)}, u32[]{:S(2)}) copy-start(bf16[1,1,4,256,128]{4,3,2,1,0:T(8,128)(2,1)} %param.8) | copy-start | bytes 786436
  3.4 0.9 %copy-start.2 = (bf16[1,1,4,256,128]{4,3,2,1,0:T(8,128)(2,1)S(1)}, bf16[1,1,4,256,128]{4,3,2,1,0:T(8,128)(2,1)}, u32[]{:S(2)}) copy-start(bf16[1,1,4,256,128]{4,3,2,1,0:T(8,128)(2,1)} %param.9) | copy-start | bytes 786436
  4.4 0.8 %copy-start.7 = (bf16[128,256]{1,0:T(8,128)(2,1)S(1)}, bf16[128,256]{1,0:T(8,128)(2,1)}, u32[]{:S(2)}) copy-start(bf16[128,256]{1,0:T(8,128)(2,1)} %down_hbm.1) | copy-start | bytes 196612
  5.2 0.8 %copy-start.8 = (bf16[256,128]{1,0:T(8,128)(2,1)S(1)}, bf16[256,128]{1,0:T(8,128)(2,1)}, u32[]{:S(2)}) copy-start(bf16[256,128]{1,0:T(8,128)(2,1)} %up_hbm.1) | copy-start | bytes 196612
  6.1 0.7 %copy-start.10 = (bf16[27,256]{1,0:T(8,128)(2,1)S(1)}, bf16[27,256]{1,0:T(8,128)(2,1)}, u32[]{:S(2)}) copy-start(bf16[27,256]{1,0:T(8,128)(2,1)} %depth_w.1) | copy-start | bytes 41476
  47.5 0.7 %copy-start.3 = (bf16[4,256,128]{2,1,0:T(8,128)(2,1)}, bf16[4,256,128]{2,1,0:T(8,128)(2,1)S(1)}, u32[]{:S(2)}) copy-start(bf16[4,256,128]{2,1,0:T(8,128)(2,1)S(1)} %get-tuple-element.15.dx) | copy-start | bytes 786436
  48.2 0.6 %copy-start.4 = (f32[128,256]{1,0:T(8,128)}, f32[128,256]{1,0:T(8,128)S(1)}, u32[]{:S(2)}) copy-start(f32[128,256]{1,0:T(8,128)S(1)} %get-tuple-element.17.dn) | copy-start | bytes 393220
  48.9 0.6 %copy-start.5 = (f32[256,128]{1,0:T(8,128)}, f32[256,128]{1,0:T(8,128)S(1)}, u32[]{:S(2)}) copy-start(f32[256,128]{1,0:T(8,128)S(1)} %get-tuple-element.19.up) | copy-start | bytes 393220
  49.5 0.6 %copy-start.6 = (f32[27,8,128]{2,1,0:T(8,128)}, f32[27,8,128]{2,1,0:T(8,128)S(1)}, u32[]{:S(2)}) copy-start(f32[27,8,128]{2,1,0:T(8,128)S(1)} %get-tuple-element.16.cw) | copy-start | bytes 331780
  50.2 0.6 %copy-start.9 = (f32[27,256]{1,0:T(8,128)}, f32[27,256]{1,0:T(8,128)S(1)}, u32[]{:S(2)}) copy-start(f32[27,256]{1,0:T(8,128)S(1)} %get-tuple-element.18.dp) | copy-start | bytes 82948

commit v3 on v2

--- a/solution.py
+++ b/solution.py
@@ -9,6 +9,7 @@
 
 F32 = jnp.float32
 BF16 = jnp.bfloat16
+GRANT = 64 * 1024 * 1024 - 128 * 1024
 HIGH = lax.Precision.HIGHEST
 DIRS = [(da, db) for da in (-1, 0, 1) for db in (-1, 0, 1) if (da, db) != (0, 0)]
 
@@ -19,12 +20,13 @@
 
 
 def level_kernel(
-    sizes, reduce, nb, nbv, depth_w, x_hbm, cot_hbm, conv_hbm, down_hbm, up_hbm,
-    dx_out, cw_out, dn_out, dp_out, up_out,
+    sizes, reduce, nb_hbm, depth_hbm, x_hbm, cot_hbm, conv_hbm, down_hbm, up_hbm,
+    dx_hbm, cw_hbm, dn_hbm, dp_hbm, up_out_hbm,
     C0, NZ, NY, NC, hz, hy, hc, sz, sy, sc, FR, T, FS, DF, WB, GA, WF,
     st10, st11, st12, rv10, rv11, rv12, st20, st21, st22, rv20, rv21, rv22,
     st30, st31, st32, rv30, rv31, rv32, ag, DG, SMALL, x_in, cot_in, conv_w, down_w, up_w,
-    hs, hr, cs, cr, p1s, p1r, p2s, p2r, p3s, p3r, gs, gr, ls,
+    nb, nbv, depth_w, dx_out, cw_out, dn_out, dp_out, up_out,
+    hs, hr, cs, cr, p1s, p1r, p2s, p2r, p3s, p3r, gs, gr, ls, os,
 ):
     B, S, H = sizes
     K = 4
@@ -45,7 +47,10 @@
         return target((blk + db) * rows + row + da)
 
     pulls = [pltpu.make_async_copy(src, dst, ls.at[i]) for i, (src, dst) in enumerate((
-        (x_hbm, x_in), (cot_hbm, cot_in), (conv_hbm, conv_w), (up_hbm, up_w), (down_hbm, down_w)))]
+        (x_hbm, x_in), (cot_hbm, cot_in), (nb_hbm, nb), (nb_hbm, nbv), (depth_hbm, depth_w),
+        (up_hbm, up_w), (down_hbm, down_w), (conv_hbm, conv_w)))]
+    pushes = [pltpu.make_async_copy(src, dst, os.at[i]) for i, (src, dst) in enumerate((
+        (dx_out, dx_hbm), (cw_out, cw_hbm), (dn_out, dn_hbm), (dp_out, dp_hbm), (up_out, up_out_hbm)))]
     for pull in pulls:
         pull.start()
 
@@ -333,7 +338,9 @@
         total = rv3[a][0].astype(F32)
         for bk in range(1, B):
             total = total + rv3[a][bk].astype(F32)
-        cw_out[9 * a:9 * a + 9] = total[0:80].reshape(10, 8, 128)[0:9]
+        cube = total[0:80].reshape(10, 8, 128)
+        for i in range(8):
+            cw_out[9 * a:9 * a + 9, 128 * i:128 * i + 128] = cube[0:9, i]
         return total
 
     if reduce:
@@ -382,12 +389,14 @@
             FS[...] += term
     for k in range(K):
         dx_out[k] = FS[:, k].reshape(256, 128).astype(BF16)
+    pushes[0].start()
 
     if reduce:
         step_sum(1)
         each(Q, lambda r: gather_in(r).wait())
         gather_pair(ch).start()
         step_sum(2)
+        pushes[1].start()
         gather_pair(1 - ch).wait()
         for c in range(2):
             for qi in range(8):
@@ -399,19 +408,24 @@
                     DG[16 * d:16 * d + 16] = ag[c, qi, 32:48].astype(F32)
         dp_out[:, :128] = DG[0:27]
         dp_out[:, 128:] = DG[32:59]
-
-
-def write_kernel(dx, cw, dn, dp, up, dx_o, cw_o, dn_o, dp_o, up_o, flat, sem):
-    moves = [pltpu.make_async_copy(src, dst, sem.at[i])
-             for i, (src, dst) in enumerate(((dx, dx_o), (dn, dn_o), (dp, dp_o), (up, up_o)))]
-    for move in moves:
-        move.start()
-    for i in range(8):
-        flat[:, 128 * i:128 * i + 128] = cw[:, i, :]
-    moves.append(pltpu.make_async_copy(flat, cw_o, sem.at[4]))
-    moves[4].start()
-    for move in moves:
-        move.wait()
+    for i, push in enumerate(pushes):
+        if i > 1 or (i == 1 and not reduce):
+            push.start()
+    for push in pushes:
+        push.wait()
+
+
+def write_kernel(*refs):
+    ins, outs, held, sem_in, sem_out = refs[0:5], refs[5:10], refs[10:15], refs[15], refs[16]
+    reads = [pltpu.make_async_copy(ins[i], held[i], sem_in.at[i]) for i in range(5)]
+    writes = [pltpu.make_async_copy(held[i], outs[i], sem_out.at[i]) for i in range(5)]
+    for read in reads:
+        read.start()
+    for read, write in zip(reads, writes):
+        read.wait()
+        write.start()
+    for write in writes:
+        write.wait()
 
 
 def per_device(
@@ -421,23 +435,22 @@
     n = B * S * H
     reduce = (B, S, H) == (4, 2, 2)
     nb = neighbours[0, 0]
-    vm = pl.BlockSpec(memory_space=pltpu.VMEM)
-    sm = pl.BlockSpec(memory_space=pltpu.SMEM)
+    hbm = pl.BlockSpec(memory_space=pltpu.HBM)
     dma = pltpu.SemaphoreType.DMA
     V = pltpu.VMEM
-    wide_rows = 8 if reduce else 128
+    taps = (27, 1024) if reduce else (27, 128, 128)
     part_rows = (128, 80, 80)
     outs = pl.pallas_call(
         functools.partial(level_kernel, mesh_sizes, reduce),
         out_shape=(
             jax.ShapeDtypeStruct((4, 256, 128), BF16),
-            jax.ShapeDtypeStruct((27, wide_rows, 128), F32),
+            jax.ShapeDtypeStruct(taps, F32),
             jax.ShapeDtypeStruct((128, 256), F32),
             jax.ShapeDtypeStruct((27, 256), F32),
             jax.ShapeDtypeStruct((256, 128), F32),
         ),
-        in_specs=[sm, vm, vm] + [pl.BlockSpec(memory_space=pl.ANY)] * 5,
-        out_specs=(vm,) * 5,
+        in_specs=[hbm] * 7,
+        out_specs=(hbm,) * 5,
         scratch_shapes=[
             V((5, 4, 8, 8, 128), F32), V((2, 5, 8, 8, 128), F32), V((2, 5, 4, 8, 128), F32),
             V((4, 5, 8, 128), F32),
@@ -456,23 +469,27 @@
             V((64, 128), F32), V((16, 48, 128), F32),
             V((4, 256, 128), BF16), V((4, 256, 128), BF16), V((27, 128, 128), BF16),
             V((128, 256), BF16), V((256, 128), BF16),
+            pltpu.SMEM((4, 27), jnp.int32), V((4, 27), jnp.int32), V((27, 256), BF16),
+            V((4, 256, 128), BF16), V(taps, F32), V((128, 256), F32), V((27, 256), F32),
+            V((256, 128), F32),
             dma((2, 8)), dma((2, 8)), dma((2, 8)), dma((2, 8)),
             dma((3,)), dma((3,)), dma((3,)), dma((3,)), dma((3, 4)), dma((3, 4)),
-            dma((8,)), dma((8,)), dma((5,)),
+            dma((8,)), dma((8,)), dma((8,)), dma((5,)),
         ],
         compiler_params=pltpu.CompilerParams(
-            collective_id=0, has_side_effects=True, vmem_limit_bytes=48 * 1024 * 1024),
+            collective_id=0, has_side_effects=True, vmem_limit_bytes=GRANT),
         name="level_pair",
-    )(nb, nb, depth_weight, fine_input[0, 0], cotangent[0, 0], conv_weight, down_weight, up_weight)
+    )(nb, depth_weight, fine_input[0, 0], cotangent[0, 0], conv_weight, down_weight, up_weight)
     dx, cw, dn, dp, up = outs
     if reduce:
-        hbm = pl.BlockSpec(memory_space=pl.ANY)
         dx, cw, dn, dp, up = pl.pallas_call(
             write_kernel,
-            out_shape=(dx, jax.ShapeDtypeStruct((27, 1024), F32), dn, dp, up),
-            in_specs=[vm] * 5,
+            out_shape=(dx, cw, dn, dp, up),
+            in_specs=[hbm] * 5,
             out_specs=(hbm,) * 5,
-            scratch_shapes=[V((27, 1024), F32), dma((5,))],
+            scratch_shapes=[V((4, 256, 128), BF16), V(taps, F32), V((128, 256), F32),
+                            V((27, 256), F32), V((256, 128), F32), dma((5,)), dma((5,))],
+            compiler_params=pltpu.CompilerParams(vmem_limit_bytes=GRANT),
             name="write_out",
         )(dx, cw, dn, dp, up)
     else:

time: 53.2 us -> 43.3 us (0.81)
  local copies, waits for them, and re-layouts: 9.37 us -> 0 us
    unnamed x24 -> x0, local copies, waits for them, and re-layouts: 9.37 us -> none
where the time goes in v3:
time: 43.3 us; the launch traced here: 43.1 us
  Pallas kernels  42.5 us (98%)
  between operations  0.64 us (1%)
    pallas_call x1, Pallas kernels, per_device(): pl.pallas_call(functools.partial(level_kernel, mesh_sizes, reduce), out_s...  40.6 us
    pallas_call x1, Pallas kernels, per_device(): pl.pallas_call(write_kernel, out_shape=(dx, cw, dn, dp, up), in_specs=[hb...  1.88 us

profile of v3, /device:TPU:0, one launch (start us, length us, event | category | flops | bytes accessed | tf_op | source)
XLA Modules:
  0.0 43.1 jit_solution(17802995484930617818)
XLA Ops:
  0.6 40.6 %level_pair.1 = (bf16[4,256,128]{2,1,0:T(8,128)(2,1)}, f32[27,1024]{1,0:T(8,128)}, f32[128,256]{1,0:T(8,128)}, f32[27,256]{1,0:T(8,128)}, f32[256,128]{1,0:T(8,128)}) custom-call(s32[4,27]{1,0:T(4,128)} %bitcast.6, bf16[27,256]{1,0:T(8,128)(2,1)} %depth_hbm.1, bf16[4,256,128]{2,1,0:T(8,128)(2,1)} %bitcast.4, bf16[4,256,128]{2,1,0:T(8,128)(2,1)} %bitcast.5, ...), custom_call_target="tpu_custom_call" | custom-call | tf_op jit(solution)/shard_map/level_pair/pallas_call | solution.py:443
  41.2 1.9 %write_out.1 = (bf16[4,256,128]{2,1,0:T(8,128)(2,1)}, f32[27,1024]{1,0:T(8,128)}, f32[128,256]{1,0:T(8,128)}, f32[27,256]{1,0:T(8,128)}, f32[256,128]{1,0:T(8,128)}) custom-call(bf16[4,256,128]{2,1,0:T(8,128)(2,1)} %get-tuple-element.15.refs_0_, f32[27,1024]{1,0:T(8,128)} %get-tuple-element.16.refs_1_, f32[128,256]{1,0:T(8,128)} %get-tuple-element.17.refs_2_, ...), custom_call_target="tpu_custom_call" | custom-call | tf_op jit(solution)/shard_map/write_out/pallas_call | solution.py:485

commit v4 on v3

--- a/solution.py
+++ b/solution.py
@@ -22,7 +22,7 @@
 def level_kernel(
     sizes, reduce, nb_hbm, depth_hbm, x_hbm, cot_hbm, conv_hbm, down_hbm, up_hbm,
     dx_hbm, cw_hbm, dn_hbm, dp_hbm, up_out_hbm,
-    C0, NZ, NY, NC, hz, hy, hc, sz, sy, sc, FR, T, FS, DF, WB, GA, WF,
+    C0, NZ, NY, NC, hz, hy, hc, sz, sy, sc, FR, T, FS, DW, WB, GA, WF,
     st10, st11, st12, rv10, rv11, rv12, st20, st21, st22, rv20, rv21, rv22,
     st30, st31, st32, rv30, rv31, rv32, ag, DG, SMALL, x_in, cot_in, conv_w, down_w, up_w,
     nb, nbv, depth_w, dx_out, cw_out, dn_out, dp_out, up_out,
@@ -215,6 +215,7 @@
             picks.append(((col == 4.0 * slot_of) & (slot_of >= 0.0) & (t < 27)).astype(F32))
     pick = jnp.concatenate(picks, axis=0).astype(BF16)
     WF[:, 9] = jnp.zeros((3, 128, 128), F32)
+    DW[...] = jnp.zeros(DW.shape, BF16)
 
     wait_halo(0)
     build()
@@ -257,7 +258,8 @@
         up_rows = cot_in[k].astype(F32).reshape(4, 2, 4, 8, 128) + wide[k].reshape(1, 2, 1, 8, 128)
         slope = silu_slope(FS[:, k]).reshape(4, 2, 4, 8, 128)
         df = (up_rows * slope * live[k]).astype(BF16)
-        DF[:, k] = df.reshape(4, 64, 128)
+        for u in range(3):
+            DW[u:u + 4, k, :, 128 * u:128 * u + 128] = df.reshape(4, 64, 128)
         C0[k] = df.astype(F32).reshape(4, 8, 8, 128)
     stage(1)
     send_halo(1)
@@ -340,7 +342,9 @@
             total = total + rv3[a][bk].astype(F32)
         cube = total[0:80].reshape(10, 8, 128)
         for i in range(8):
-            cw_out[9 * a:9 * a + 9, 128 * i:128 * i + 128] = cube[0:9, i]
+            for u in range(3):
+                cw_out[9 * u + 3 * a:9 * u + 3 * a + 3, 128 * i:128 * i + 128] = (
+                    cube[3 * u:3 * u + 3, i])
         return total
 
     if reduce:
@@ -359,17 +363,21 @@
         dp_out[:, 128:] = DG[32:59]
 
     for a in range(3):
-        wg = lax.dot_general(T[a:a + 4].reshape(1024, 1152), DF[...].reshape(1024, 128),
+        wg = lax.dot_general(T[:, :, :, 384 * a:384 * a + 384].reshape(1536, 384),
+                             DW[...].reshape(1536, 384),
                              (((0,), (0,)), ((), ())), preferred_element_type=F32)
         if reduce:
-            WF[a, 0:9] = wg.reshape(9, 128, 128)
+            for u in range(3):
+                WF[a, 3 * u:3 * u + 3] = wg[:, 128 * u:128 * u + 128].reshape(3, 128, 128)
             step_core(a)
             if a > 0:
                 step_slab(a - 1)
             if a > 1:
                 step_blk(a - 2)
         else:
-            cw_out[9 * a:9 * a + 9] = wg.reshape(9, 128, 128)
+            for u in range(3):
+                cw_out[9 * u + 3 * a:9 * u + 3 * a + 3] = (
+                    wg[:, 128 * u:128 * u + 128].reshape(3, 128, 128))
     if reduce:
         step_slab(2)
         step_blk(1)
@@ -457,7 +465,7 @@
             V((2, 2, 256, 128), BF16), V((2, 2, 128, 128), BF16), V((2, 4, 32, 128), BF16),
             V((2, 2, 256, 128), BF16), V((2, 2, 128, 128), BF16), V((2, 4, 32, 128), BF16),
             V((3, 6, 10, 8, 128), F32), V((6, 4, 64, 1152), BF16), V((4, 4, 64, 128), F32),
-            V((4, 4, 64, 128), BF16), V((3, 1152, 128), BF16), V((2, 9, 16, 256), BF16),
+            V((6, 4, 64, 384), BF16), V((3, 1152, 128), BF16), V((2, 9, 16, 256), BF16),
             V((3, 10, 128, 128), F32),
             *[V((2, B, rows, 128), BF16) for rows in part_rows],
             *[V((2, B, rows, 128), BF16) for rows in part_rows],

time: 43.3 us -> 42.3 us (0.977)
  Pallas kernels: 42.5 us -> 41.5 us
    pallas_call x1, Pallas kernels: 40.6 us -> 39.6 us  [per_device(): pl.pallas_call(functools.partial(level_kernel, mesh_sizes, reduce), out_s...]
where the time goes in v4:
time: 42.3 us; the launch traced here: 42.1 us
  Pallas kernels  41.5 us (98%)
  between operations  0.64 us (2%)
    pallas_call x1, Pallas kernels, per_device(): pl.pallas_call(functools.partial(level_kernel, mesh_sizes, reduce), out_s...  39.6 us
    pallas_call x1, Pallas kernels, per_device(): pl.pallas_call(write_kernel, out_shape=(dx, cw, dn, dp, up), in_specs=[hb...  1.88 us

profile of v4, /device:TPU:0, one launch (start us, length us, event | category | flops | bytes accessed | tf_op | source)
XLA Modules:
  0.0 42.1 jit_solution(16733242284637503812)
XLA Ops:
  0.6 39.6 %level_pair.1 = (bf16[4,256,128]{2,1,0:T(8,128)(2,1)}, f32[27,1024]{1,0:T(8,128)}, f32[128,256]{1,0:T(8,128)}, f32[27,256]{1,0:T(8,128)}, f32[256,128]{1,0:T(8,128)}) custom-call(s32[4,27]{1,0:T(4,128)} %bitcast.6, bf16[27,256]{1,0:T(8,128)(2,1)} %depth_hbm.1, bf16[4,256,128]{2,1,0:T(8,128)(2,1)} %bitcast.4, bf16[4,256,128]{2,1,0:T(8,128)(2,1)} %bitcast.5, ...), custom_call_target="tpu_custom_call" | custom-call | tf_op jit(solution)/shard_map/level_pair/pallas_call | solution.py:451
  40.2 1.9 %write_out.1 = (bf16[4,256,128]{2,1,0:T(8,128)(2,1)}, f32[27,1024]{1,0:T(8,128)}, f32[128,256]{1,0:T(8,128)}, f32[27,256]{1,0:T(8,128)}, f32[256,128]{1,0:T(8,128)}) custom-call(bf16[4,256,128]{2,1,0:T(8,128)(2,1)} %get-tuple-element.15.refs_0_, f32[27,1024]{1,0:T(8,128)} %get-tuple-element.16.refs_1_, f32[128,256]{1,0:T(8,128)} %get-tuple-element.17.refs_2_, ...), custom_call_target="tpu_custom_call" | custom-call | tf_op jit(solution)/shard_map/write_out/pallas_call | solution.py:493
